TPU v7x, 512 devices: a whole 4x4x16 slice. The times are simulated.
512 devices in a mesh: dec: 128 (over x, z, core), tp: 4 (over y).
Axes of the slice: x: 4, y: 4, z: 16, core: 2. Of those that a mesh axis runs over, the one named last changes fastest.
Arguments:
- hidden_rows: bfloat16 [8, 18432, 7168], P(None, 'dec', 'tp')
- compress_weight: bfloat16 [7168, 576], P('tp')
- latent_gain: float32 [512], replicated, may hold values from 0.25 to 1.75
- segment_page: int32 [18432], replicated, may hold values from 0 to 18431, as said below
- segment_length: int32 [18432], replicated, may hold values from 1 to 8, as said below
- segment_start: int32 [18432], replicated, may hold values from 0 to 4088, as said below
Outputs:
- latent_cache: bfloat16 [8, 18432, 576], P('tp', 'dec')
Inputs may be any that keep to these rules, and one draw needn't show every extreme that they name: `segment_page`: a permutation of the pages. Segment s is loaded on dec index s // 144, and its page belongs to the owner segment_page[s] // 144, so every owner receives exactly 144 segments. No dec index loads more than 2 segments for one owner, and some loads exactly 2. `segment_length`: some segment has all 8 rows live. `segment_start`: multiples of 8.
All inputs are finite; a program needn't handle non-finite values.
Results may differ from a plain program's by a relative error of at most 0.0012.
Values may be sent and summed in bfloat16 or wider, within the bound.
A program may use at most 64 MiB of HBM per device.

v0:
```python
import jax
import jax.numpy as jnp
from jax import lax
from jax.sharding import PartitionSpec as P


def finish_rows(projected, latent_gain, position):
    rank_width = latent_gain.shape[0]
    latent = projected[..., :rank_width]
    rotary = projected[..., rank_width:]
    mean_square = jnp.mean(latent * latent, axis=-1, keepdims=True)
    latent = latent / jnp.sqrt(mean_square + 1e-06) * latent_gain
    half_width = rotary.shape[-1] // 2
    exponent = jnp.arange(half_width, dtype=jnp.float32) * (2.0 / rotary.shape[-1])
    frequency = jnp.power(jnp.float32(10000.0), -exponent)
    phase_angle = position[..., None] * frequency
    cosine = jnp.cos(phase_angle)
    sine_part = jnp.sin(phase_angle)
    front_half = rotary[..., :half_width]
    back_half = rotary[..., half_width:]
    return jnp.concatenate(
        [
            latent,
            front_half * cosine - back_half * sine_part,
            back_half * cosine + front_half * sine_part,
        ],
        axis=-1,
    )


def owner_layout(segment_page, segment_length, segments_each, capacity, own_index):
    loaders = segment_page.shape[0] // segments_each
    page_owner = segment_page // segments_each
    bound_here = (page_owner == own_index).astype(jnp.int32).reshape(loaders, segments_each)
    earlier = jnp.cumsum(bound_here, axis=1) - bound_here
    slot_all = (jnp.arange(loaders, dtype=jnp.int32)[:, None] * capacity + earlier).reshape(-1)
    own_pages = own_index * segments_each + jnp.arange(segments_each, dtype=jnp.int32)
    matches = segment_page[:, None] == own_pages[None, :]
    page_slot = jnp.sum(jnp.where(matches, slot_all[:, None], 0), axis=0)
    page_length = jnp.sum(jnp.where(matches, segment_length[:, None], 0), axis=0)
    return (page_slot, page_length)


def loader_slots(segment_page, segments_each, capacity, own_index, loaders):
    own_pages = lax.dynamic_slice_in_dim(segment_page, own_index * segments_each, segments_each)
    target = own_pages // segments_each
    onehot = (target[:, None] == jnp.arange(loaders, dtype=jnp.int32)[None, :]).astype(jnp.int32)
    earlier = jnp.cumsum(onehot, axis=0) - onehot
    return target * capacity + jnp.sum(onehot * earlier, axis=1)


def shards(hidden_rows, compress_weight, latent_gain, segment_page, segment_length, segment_start):
    loaders = lax.axis_size("dec")
    tensor_ways = lax.axis_size("tp")
    own_index = lax.axis_index("dec")
    tensor_index = lax.axis_index("tp")
    seg_rows, segments_each, width_part = hidden_rows.shape
    capacity = max(2, (segments_each + loaders - 1) // loaders)
    quarter = seg_rows // tensor_ways
    page_slot, page_length = owner_layout(
        segment_page, segment_length, segments_each, capacity, own_index
    )
    row_offset = tensor_index * quarter + jnp.arange(quarter, dtype=jnp.int32)
    live_rows = row_offset[:, None] < page_length[None, :]
    send_slots = loader_slots(segment_page, segments_each, capacity, own_index, loaders)
    slot_ids = jnp.arange(loaders * capacity, dtype=jnp.int32)
    partial_sums = jnp.einsum(
        "rsd,dl->rsl", hidden_rows, compress_weight, preferred_element_type=jnp.float32
    )
    summed = lax.psum(partial_sums, "tp")
    projected = lax.dynamic_slice_in_dim(summed, tensor_index * quarter, quarter, 0)
    own_starts = lax.dynamic_slice_in_dim(segment_start, own_index * segments_each, segments_each)
    position = (own_starts[None, :] + row_offset[:, None]).astype(jnp.float32)
    computed = finish_rows(projected, latent_gain, position).astype(jnp.bfloat16)
    send_table = (slot_ids[:, None] == send_slots[None, :]).astype(jnp.bfloat16)
    outgoing = jnp.einsum(
        "ts,rsl->rtl", send_table, computed, preferred_element_type=jnp.float32
    ).astype(jnp.bfloat16)
    arrived = lax.all_to_all(outgoing, "dec", split_axis=1, concat_axis=1, tiled=True)
    receive_table = (page_slot[:, None] == slot_ids[None, :]).astype(jnp.bfloat16)
    finished = jnp.einsum(
        "jt,rtl->rjl", receive_table, arrived, preferred_element_type=jnp.float32
    ).astype(jnp.bfloat16)
    return jnp.where(live_rows[:, :, None], finished, jnp.zeros_like(finished))


def solution(mesh):
    in_specs = (P(None, "dec", "tp"), P("tp", None), P(), P(), P(), P())
    out_specs = P("tp", "dec", None)
    return jax.shard_map(shards, mesh=mesh, in_specs=in_specs, out_specs=out_specs, check_vma=False)
```

profile of v0, /device:TPU:1, one launch (start us, length us, event | category | flops | bytes accessed | tf_op | source)
XLA Modules:
  0.0 207.6 jit_solution(10635883227692239150)
XLA Ops:
  6.5 0.0 copy-start
  6.5 0.0 all-reduce.4.cloned.1.call-start
  6.5 1.6 copy-done
  8.1 8.2 %fusion.2 = f32[8,144,576]{1,2,0:T(8,128)} fusion(bf16[8,144,1792]{2,1,0:T(8,128)(2,1)} %param.6, bf16[1792,576]{0,1:T(8,128)(2,1)S(1)} %copy-done), kind=kOutput, calls=%fused_computation.4 | convolution fusion | flops 2378170368 | bytes 8847360 | tf_op jit(solution)/shard_map/rsd,dl->rsl/dot_general | solution.py:67
  16.3 0.0 copy-start.1
  16.3 0.0 copy-start.3
  16.3 0.0 all-reduce.4.cloned.1.call-update
  16.3 0.8 dynamic_slice.10
  17.1 0.1 copy-done.1
  17.2 0.1 and_select_fusion
  17.3 0.1 iota_compare_fusion.2
  17.4 0.1 fusion.19
  17.7 0.2 fusion.27
  17.8 0.1 multiply_add_fusion
  17.9 0.1 add_convert_fusion
  18.0 120.6 %all-reduce.4.cloned.1.call-done = f32[8,144,576]{1,2,0:T(8,128)} async-done(((f32[8,144,576]{1,2,0:T(8,128)}), f32[8,144,576]{1,2,0:T(8,128)}) %all-reduce.4.cloned.1.call-update) | async-done | bytes 2654224 | tf_op jit(solution)/shard_map/psum | solution.py:70
  138.6 1.3 multiply_reduce_fusion
  139.9 0.0 copy-done.3
  140.0 0.0 copy-start.2
  140.0 1.4 multiply_convert_fusion
  141.4 1.2 fusion.33
  142.6 0.4 fusion.4
  143.0 1.8 copy.33
  144.8 16.6 %all-to-all-start = ((bf16[2,256,576]{2,0,1:T(2,128)(2,1)}), bf16[2,256,576]{2,0,1:T(2,128)(2,1)S(1)}, u32[]{:S(2)}, u32[]{:S(2)}) async-start(bf16[2,256,576]{2,0,1:T(2,128)(2,1)} %copy.33), calls=%async_computation | async-start | bytes 1310720 | tf_op jit(solution)/shard_map/all_to_all | solution.py:79
  161.4 0.1 fusion.31
  161.5 0.1 reshape.122
  161.6 0.1 copy.42
  161.7 0.1 fusion.17
  162.0 0.1 copy.41
  162.1 0.1 subtract_add_fusion
  162.2 0.1 broadcast_in_dim.30
  162.3 0.0 copy-done.2
  162.3 3.2 %fusion.1 = (s32[144]{0:T(256)S(1)}, s32[144]{0:T(256)S(1)}) fusion(s32[18432]{0:T(1024)S(1)} %broadcast_in_dim.30, s32[18432]{0:T(1024)S(1)} %copy-done.1, s32[144]{0:T(256)S(1)} %iota_add_fusion, s32[18432]{0:T(1024)S(1)} %copy-done.2), kind=kLoop, calls=%fused_computation.3 | loop fusion | flops 13270752 | bytes 222912 | tf_op jit(solution)/shard_map/reduce_sum | solution.py:39
  165.6 0.1 broadcast_compare_fusion
  165.7 34.1 %all-to-all-done = bf16[2,256,576]{2,0,1:T(2,128)(2,1)S(1)} async-done(((bf16[2,256,576]{2,0,1:T(2,128)(2,1)}), bf16[2,256,576]{2,0,1:T(2,128)(2,1)S(1)}, u32[]{:S(2)}, u32[]{:S(2)}) %all-to-all-start) | async-done | bytes 589856 | tf_op jit(solution)/shard_map/all_to_all | solution.py:79
  199.7 1.1 fusion.6
  (20 shorter events, 0.2 us)
Async XLA Ops:
  6.5 1.6 copy-start
  6.5 132.1 %all-reduce.4.cloned.1.call-start = ((), (), s32[]{:S(2)}) async-start(), calls=%async_computation.1 | async-start | bytes 9437184 | tf_op jit(solution)/shard_map/psum | solution.py:70
  16.3 0.9 copy-start.1
  16.3 123.6 %copy-start.3 = (f32[512]{0:T(512)S(1)}, f32[512]{0:T(512)}, u32[]{:S(2)}) copy-start(f32[512]{0:T(512)} %param.8) | copy-start | bytes 6148
  140.0 22.4 %copy-start.2 = (s32[18432]{0:T(1024)S(1)}, s32[18432]{0:T(1024)}, u32[]{:S(2)}) copy-start(s32[18432]{0:T(1024)} %param.10) | copy-start | bytes 221188
  144.8 54.9 %all-to-all-start = ((bf16[2,256,576]{2,0,1:T(2,128)(2,1)}), bf16[2,256,576]{2,0,1:T(2,128)(2,1)S(1)}, u32[]{:S(2)}, u32[]{:S(2)}) async-start(bf16[2,256,576]{2,0,1:T(2,128)(2,1)} %copy.33), calls=%async_computation | async-start | bytes 1310720 | tf_op jit(solution)/shard_map/all_to_all | solution.py:79
Sparse Core Ops, SparseCore 0:
  16.5 122.0 all-reduce.3
where the time goes:
time: 208 us
  waiting for transfers between devices  155 us (75%)
  starting transfers between devices  16.6 us (8%)
  between operations  13.6 us (7%)
  matrix products  9.63 us (5%)
  other arithmetic  8.36 us (4%)
  local copies, waits for them, and re-layouts  4.77 us (2%)
    psum x1, waiting for transfers between devices, shards(): summed = lax.psum(partial_sums, 'tp')  121 us
    all_to_all x1, waiting for transfers between devices, shards(): lax.all_to_all(outgoing, 'dec', split_axis=1, concat_axis=1, tiled=True)  34.1 us
    all_to_all x1, starting transfers between devices, shards(): lax.all_to_all(outgoing, 'dec', split_axis=1, concat_axis=1, tiled=True)  16.6 us
    dot_general x1, matrix products, shards(): jnp.einsum('rsd,dl->rsl', hidden_rows, compress_weight, preferred_element...  8.2 us
  transfers between devices with their start and end apart: 2, of which 2 were waited for; matrix products, arithmetic and copies ran while one was open for 3% of the time, Pallas kernels for 0%

commit v1 on v0

v1 whole, which is shorter than its diff:
```python
import functools

import jax
import jax.numpy as jnp
from jax import lax
from jax.experimental import pallas as pl
from jax.experimental.pallas import tpu as pltpu
from jax.sharding import PartitionSpec as P

MESH = pl.DeviceIdType.MESH
TP = 4
NZ = 16
NQ = 8
CAP = 2
SEGS_EACH = 144
RANK = 512
LAT = 576
META = 64
HALF_A = 72
INV_SEGS = 7282


def first_axis_iota(rows, columns):
    return lax.broadcasted_iota(jnp.int32, (rows, columns), 0)


def last_axis_iota(rows, columns):
    return lax.broadcasted_iota(jnp.int32, (rows, columns), 1)


def as_column(row):
    n = row.shape[1]
    same = first_axis_iota(n, n) == last_axis_iota(n, n)
    return jnp.sum(jnp.where(same, row, 0.0), axis=1, keepdims=True)


def as_row(column):
    n = column.shape[0]
    same = first_axis_iota(n, n) == last_axis_iota(n, n)
    return jnp.sum(jnp.where(same, column, 0.0), axis=0, keepdims=True)


def own_entries(ref, own_index):
    offset = own_index * SEGS_EACH
    top = offset // 128
    lane = offset % 128
    first = ref[pl.ds(top, 1), :]
    second = ref[pl.ds(top + 1, 1), :]
    both = jnp.concatenate([first, second], axis=1)
    rolled = pltpu.roll(both, (256 - lane) % 256, axis=1)
    return rolled[:, :SEGS_EACH]


def kernel(
    x_hbm, w_hbm, gain_ref, page_hbm, length_hbm, start_hbm, freq_ref, out_ref,
    x_buf, w_buf, page_buf, length_buf, start_buf,
    part, opp_a, opp_b, from_left, from_right,
    z_send0, z_send1, z_recv0, z_recv1, p_send0, p_send1, p_recv0, p_recv1,
    x_sem, w_sem, i_sem, ys, yr, zs, zr, ps, pr,
):
    dec = lax.axis_index("dec")
    tp = lax.axis_index("tp")
    core = dec % 2
    z = (dec // 2) % NZ
    xx = dec // (2 * NZ)
    plane = xx * 2 + core
    left = (tp + TP - 1) % TP
    right = (tp + 1) % TP
    z_send, z_recv = (z_send0, z_send1), (z_recv0, z_recv1)
    p_send, p_recv = (p_send0, p_send1), (p_recv0, p_recv1)

    def z_device(zz):
        return xx * (2 * NZ) + zz * 2 + core

    def p_device(qq):
        return (qq // 2) * (2 * NZ) + z * 2 + qq % 2

    targets = ((tp + 2) % TP, right, left, tp)
    w_copy = pltpu.make_async_copy(w_hbm, w_buf, w_sem)
    w_copy.start()
    x_copies = [
        pltpu.make_async_copy(x_hbm.at[pl.ds(2 * target, 2)], x_buf.at[i], x_sem.at[i])
        for i, target in enumerate(targets)
    ]
    for copy in x_copies:
        copy.start()
    index_copies = [
        pltpu.make_async_copy(src, dst, i_sem.at[i])
        for i, (src, dst) in enumerate(
            ((page_hbm, page_buf), (length_hbm, length_buf), (start_hbm, start_buf))
        )
    ]
    for copy in index_copies:
        copy.start()

    barrier = pltpu.get_barrier_semaphore()
    for neighbour in (left, right):
        pl.semaphore_signal(barrier, inc=1, device_id=(dec, neighbour), device_id_type=MESH)

    def greet_z(i, carry):
        pl.semaphore_signal(
            barrier, inc=1, device_id=(z_device((z + i) % NZ), tp), device_id_type=MESH
        )
        return carry

    def greet_p(i, carry):
        pl.semaphore_signal(
            barrier, inc=1, device_id=(p_device((plane + i) % NQ), tp), device_id_type=MESH
        )
        return carry

    lax.fori_loop(1, NZ, greet_z, 0)
    lax.fori_loop(1, NQ, greet_p, 0)

    def project(i):
        x_copies[i].wait()
        block = x_buf[i].reshape(2 * SEGS_EACH, x_buf.shape[-1])
        result = jnp.dot(block, w_buf[...], preferred_element_type=jnp.float32)
        part[i] = result.reshape(2, SEGS_EACH, LAT)

    def y_copy(src, dst, rho, kind, target):
        return pltpu.make_async_remote_copy(
            src_ref=src,
            dst_ref=dst,
            send_sem=ys.at[rho, kind],
            recv_sem=yr.at[rho, kind],
            device_id=(dec, target),
            device_id_type=MESH,
        )

    rows_a = pl.ds(0, HALF_A)
    rows_b = pl.ds(HALF_A, SEGS_EACH - HALF_A)
    y_copies = [
        [
            y_copy(part.at[0, rho, rows_a], opp_a.at[rho], rho, 0, right),
            y_copy(part.at[0, rho, rows_b], opp_b.at[rho], rho, 1, left),
            y_copy(part.at[1, rho, rows_b], from_left.at[rho, rows_b], rho, 2, right),
            y_copy(part.at[2, rho, rows_a], from_right.at[rho, rows_a], rho, 3, left),
            y_copy(part.at[1, rho, rows_a], from_left.at[rho, rows_a], rho, 4, right),
            y_copy(part.at[2, rho, rows_b], from_right.at[rho, rows_b], rho, 5, left),
        ]
        for rho in range(2)
    ]

    w_copy.wait()
    project(0)
    pl.semaphore_wait(barrier, 2 + (NZ - 1) + (NQ - 1))
    y_copies[0][0].start()
    y_copies[0][1].start()
    project(1)
    y_copies[0][2].start()
    project(2)
    y_copies[0][3].start()
    y_copies[1][0].start()
    y_copies[1][1].start()
    project(3)

    for copy in index_copies:
        copy.wait()
    page_row = own_entries(page_buf, dec)
    length_row = own_entries(length_buf, dec)
    start_row = own_entries(start_buf, dec)
    owner_row = (page_row * INV_SEGS) >> 20
    place_row = page_row - owner_row * SEGS_EACH
    length_col = as_column(length_row.astype(jnp.float32))
    start_col = as_column(start_row.astype(jnp.float32))
    place_col = as_column(place_row.astype(jnp.float32))
    owner_col = as_column(owner_row.astype(jnp.float32))
    same_owner = owner_col == owner_row.astype(jnp.float32)
    is_earlier = first_axis_iota(SEGS_EACH, SEGS_EACH) < last_axis_iota(SEGS_EACH, SEGS_EACH)
    earlier_row = jnp.sum(
        jnp.where(same_owner, jnp.where(is_earlier, 1.0, 0.0), 0.0), axis=0, keepdims=True
    ).astype(jnp.int32)
    owner_plane = (owner_row >> 5) * 2 + (owner_row & 1)
    owner_z = (owner_row >> 1) & (NZ - 1)
    slot_row = owner_z * (NQ * CAP) + owner_plane * CAP + earlier_row
    slots = NZ * NQ * CAP
    send_table = jnp.where(
        first_axis_iota(slots, SEGS_EACH) == slot_row, 1.0, 0.0
    ).astype(jnp.bfloat16)
    meta = jnp.broadcast_to(place_col + 1.0, (SEGS_EACH, META))

    out_slot = first_axis_iota(slots, slots)
    in_slot = last_axis_iota(slots, slots)
    wanted = ((out_slot >> 1) & (NZ - 1)) * (NQ * CAP) + (out_slot >> 5) * CAP + (out_slot & 1)
    turn_table = jnp.where(wanted == in_slot, 1.0, 0.0).astype(jnp.bfloat16)

    angles = []
    for rho in range(2):
        position = start_col + (2 * tp + rho).astype(jnp.float32)
        phase = position * freq_ref[...]
        angles.append((jnp.cos(phase), jnp.sin(phase)))

    def add_and_pass(rho):
        y_copies[rho][0].wait_recv()
        part[1, rho, rows_a] = part[1, rho, rows_a] + opp_a[rho]
        y_copies[rho][4].start()
        y_copies[rho][1].wait_recv()
        part[2, rho, rows_b] = part[2, rho, rows_b] + opp_b[rho]
        y_copies[rho][5].start()

    add_and_pass(0)
    y_copies[1][2].start()
    y_copies[1][3].start()
    add_and_pass(1)

    def z_copy(rho, other):
        return pltpu.make_async_remote_copy(
            src_ref=z_send[rho].at[other],
            dst_ref=z_recv[rho].at[z],
            send_sem=zs.at[rho, other],
            recv_sem=zr.at[rho, z],
            device_id=(z_device(other), tp),
            device_id_type=MESH,
        )

    def z_arrival(rho, other):
        return pltpu.make_async_remote_copy(
            src_ref=z_send[rho].at[other],
            dst_ref=z_recv[rho].at[other],
            send_sem=zs.at[rho, other],
            recv_sem=zr.at[rho, other],
            device_id=(z_device(other), tp),
            device_id_type=MESH,
        )

    def p_copy(rho, other):
        return pltpu.make_async_remote_copy(
            src_ref=p_send[rho].at[other],
            dst_ref=p_recv[rho].at[plane],
            send_sem=ps.at[rho, other],
            recv_sem=pr.at[rho, plane],
            device_id=(p_device(other), tp),
            device_id_type=MESH,
        )

    def p_arrival(rho, other):
        return pltpu.make_async_remote_copy(
            src_ref=p_send[rho].at[other],
            dst_ref=p_recv[rho].at[other],
            send_sem=ps.at[rho, other],
            recv_sem=pr.at[rho, other],
            device_id=(p_device(other), tp),
            device_id_type=MESH,
        )

    def each(count, me, act):
        def step(i, carry):
            act((me + i) % count)
            return carry

        lax.fori_loop(1, count, step, 0)

    def finish(rho):
        for kind in (2, 3, 4, 5):
            y_copies[rho][kind].wait_recv()
        total = part[3, rho] + from_left[rho] + from_right[rho]
        latent = total[:, :RANK]
        rotary = total[:, RANK:]
        mean_square = jnp.sum(latent * latent, axis=1, keepdims=True) * (1.0 / RANK)
        latent = latent / jnp.sqrt(mean_square + 1e-06) * gain_ref[...]
        half = (LAT - RANK) // 2
        front, back = rotary[:, :half], rotary[:, half:]
        cosine, sine = angles[rho]
        pieces = [latent, front * cosine - back * sine, back * cosine + front * sine]
        row = jnp.concatenate(pieces, axis=1)
        alive = (2 * tp + rho).astype(jnp.float32) < length_col
        row = jnp.where(alive, row, 0.0)
        if rho == 0:
            row = jnp.concatenate([row, meta], axis=1)
        sent = jnp.dot(send_table, row.astype(jnp.bfloat16), preferred_element_type=jnp.float32)
        z_send[rho][...] = sent.astype(jnp.bfloat16).reshape(z_send[rho].shape)
        z_recv[rho][z] = z_send[rho][z]
        each(NZ, z, lambda other: z_copy(rho, other).start())

    def turn(rho):
        each(NZ, z, lambda other: z_arrival(rho, other).wait_recv())
        arrived = z_recv[rho][...].reshape(slots, z_recv[rho].shape[-1])
        turned = jnp.dot(turn_table, arrived, preferred_element_type=jnp.float32)
        p_send[rho][...] = turned.astype(jnp.bfloat16).reshape(p_send[rho].shape)
        p_recv[rho][plane] = p_send[rho][plane]
        each(NQ, plane, lambda other: p_copy(rho, other).start())

    finish(0)
    finish(1)
    turn(0)
    turn(1)
    each(NQ, plane, lambda other: p_arrival(0, other).wait_recv())
    landed = p_recv0[...].reshape(slots, LAT + META)
    place = as_row(landed[:, LAT : LAT + 1].astype(jnp.float32))
    page_ids = (first_axis_iota(SEGS_EACH, slots) + 1).astype(jnp.float32)
    take_table = jnp.where(page_ids == place, 1.0, 0.0).astype(jnp.bfloat16)
    out_ref[0] = jnp.dot(
        take_table, landed[:, :LAT], preferred_element_type=jnp.float32
    ).astype(jnp.bfloat16)
    each(NQ, plane, lambda other: p_arrival(1, other).wait_recv())
    out_ref[1] = jnp.dot(
        take_table, p_recv1[...].reshape(slots, LAT), preferred_element_type=jnp.float32
    ).astype(jnp.bfloat16)

    for rho in range(2):
        for copy in y_copies[rho]:
            copy.wait_send()
        each(NZ, z, lambda other: z_copy(rho, other).wait_send())
        each(NQ, plane, lambda other: p_copy(rho, other).wait_send())


def shards(hidden_rows, compress_weight, latent_gain, segment_page, segment_length, segment_start):
    half = (LAT - RANK) // 2
    exponent = jnp.arange(half, dtype=jnp.float32) * (2.0 / (LAT - RANK))
    frequency = jnp.power(jnp.float32(10000.0), -exponent).reshape(1, half)
    width = hidden_rows.shape[-1]
    any_spec = pl.BlockSpec(memory_space=pltpu.HBM)
    vmem_spec = pl.BlockSpec(memory_space=pltpu.VMEM)
    dma = pltpu.SemaphoreType.DMA
    bf16, f32 = jnp.bfloat16, jnp.float32
    n = SEGS_EACH
    scratch = [
        pltpu.VMEM((TP, 2, n, width), bf16),
        pltpu.VMEM((width, LAT), bf16),
        pltpu.VMEM((n, 128), jnp.int32),
        pltpu.VMEM((n, 128), jnp.int32),
        pltpu.VMEM((n, 128), jnp.int32),
        pltpu.VMEM((TP, 2, n, LAT), f32),
        pltpu.VMEM((2, HALF_A, LAT), f32),
        pltpu.VMEM((2, n - HALF_A, LAT), f32),
        pltpu.VMEM((2, n, LAT), f32),
        pltpu.VMEM((2, n, LAT), f32),
        pltpu.VMEM((NZ, NQ * CAP, LAT + META), bf16),
        pltpu.VMEM((NZ, NQ * CAP, LAT), bf16),
        pltpu.VMEM((NZ, NQ * CAP, LAT + META), bf16),
        pltpu.VMEM((NZ, NQ * CAP, LAT), bf16),
        pltpu.VMEM((NQ, NZ * CAP, LAT + META), bf16),
        pltpu.VMEM((NQ, NZ * CAP, LAT), bf16),
        pltpu.VMEM((NQ, NZ * CAP, LAT + META), bf16),
        pltpu.VMEM((NQ, NZ * CAP, LAT), bf16),
        dma((TP,)),
        dma(()),
        dma((3,)),
        dma((2, 6)),
        dma((2, 6)),
        dma((2, NZ)),
        dma((2, NZ)),
        dma((2, NQ)),
        dma((2, NQ)),
    ]
    return pl.pallas_call(
        kernel,
        out_shape=jax.ShapeDtypeStruct((2, n, LAT), bf16),
        in_specs=[any_spec, any_spec, vmem_spec, any_spec, any_spec, any_spec, vmem_spec],
        out_specs=vmem_spec,
        scratch_shapes=scratch,
        compiler_params=pltpu.CompilerParams(
            collective_id=0, has_side_effects=True, vmem_limit_bytes=50 * 1024 * 1024
        ),
        cost_estimate=pl.CostEstimate(
            flops=2 * 8 * n * width * LAT, bytes_accessed=7_000_000, transcendentals=0
        ),
        name="latent_rows",
    )(
        hidden_rows,
        compress_weight,
        latent_gain.reshape(1, RANK),
        segment_page.reshape(n, 128),
        segment_length.reshape(n, 128),
        segment_start.reshape(n, 128),
        frequency,
    )


def solution(mesh):
    in_specs = (P(None, "dec", "tp"), P("tp", None), P(), P(), P(), P())
    out_specs = P("tp", "dec", None)
    return jax.shard_map(shards, mesh=mesh, in_specs=in_specs, out_specs=out_specs, check_vma=False)
```

time: 208 us -> 78.2 us (0.38)
  waiting for transfers between devices: 155 us -> 0 us
  Pallas kernels: 0 us -> 74 us
  starting transfers between devices: 16.6 us -> 0 us
  between operations: 13.6 us -> 0.06 us
  matrix products: 9.63 us -> 0 us
  other arithmetic: 8.36 us -> 0.01 us
    psum x1 -> x0, waiting for transfers between devices: 121 us -> none  [shards(): summed = lax.psum(partial_sums, 'tp')]
    pallas_call x0 -> x1, Pallas kernels: none -> 74 us  [shards(): pl.pallas_call(kernel, out_shape=jax.ShapeDtypeStruct((2, n, LAT), bf16),...]
    all_to_all x1 -> x0, waiting for transfers between devices: 34.1 us -> none  [shards(): lax.all_to_all(outgoing, 'dec', split_axis=1, concat_axis=1, tiled=True)]
    all_to_all x1 -> x0, starting transfers between devices: 16.6 us -> none  [shards(): lax.all_to_all(outgoing, 'dec', split_axis=1, concat_axis=1, tiled=True)]
    dot_general x3 -> x0, matrix products: 9.63 us -> none  [the longest x1 8.2 us: shards(): jnp.einsum('rsd,dl->rsl', hidden_rows, compress_weight, preferred_element...]
    reduce_sum x3 -> x0, other arithmetic: 4.76 us -> none  [the longest x1 3.23 us: owner_layout(): page_slot = jnp.sum(jnp.where(matches, slot_all[:, None], 0), axis=0)]
    another operation x9 -> x0, other arithmetic: 3.01 us -> none
    unnamed x12 -> x10, local copies, waits for them, and re-layouts: 1.85 us -> 3.98 us
  transfers between devices with their start and end apart: 2 -> 0, of which waited for: 2 -> 0; matrix products, arithmetic and copies ran while one was open for 3% -> 0% of each run, Pallas kernels for 0% -> 0%
where the time goes in v1:
time: 78.2 us; the launch traced here: 78 us
  Pallas kernels  74 us (95%)
  local copies, waits for them, and re-layouts  3.98 us (5%)
    pallas_call x1, Pallas kernels, shards(): pl.pallas_call(kernel, out_shape=jax.ShapeDtypeStruct((2, n, LAT), bf16),...  74 us
    unnamed x10, local copies, waits for them, and re-layouts  3.98 us

profile of v1, /device:TPU:1, one launch (start us, length us, event | category | flops | bytes accessed | tf_op | source)
XLA Modules:
  0.0 78.0 jit_solution(6358094945956609118)
XLA Ops:
  0.0 0.0 copy-start.2
  0.0 0.0 copy-start.1
  0.0 0.0 copy-start
  0.0 0.0 copy-start.3
  0.0 3.2 %copy.7.w_hbm = bf16[1792,576]{1,0:T(8,128)(2,1)S(1)} copy(bf16[1792,576]{0,1:T(8,128)(2,1)} %param.7) | data formatting | bytes 4128768 | tf_op args[1]
  3.3 0.0 copy-done.2
  3.3 0.0 copy-done.1
  3.3 0.0 copy-done
  3.3 0.0 copy-done.3
  3.3 74.0 %latent_rows.1 = bf16[2,144,576]{2,1,0:T(8,128)(2,1)S(1)} custom-call(bf16[8,144,1792]{2,1,0:T(8,128)(2,1)} %x_hbm.1, bf16[1792,576]{1,0:T(8,128)(2,1)S(1)} %copy.7.w_hbm, f32[1,512]{1,0:T(1,128)S(1)} %bitcast.7, s32[144,128]{1,0:T(8,128)S(1)} %bitcast.4, s32[144,128]{1,0:T(8,128)S(1)} %bitcast.5, s32[144,128]{1,0:T(8,128)S(1)} %bitcast.6, ...), custom_call_target="tpu_custom_call" | custom-call | flops 2378170368 | bytes 7000000 | tf_op jit(solution)/shard_map/latent_rows/pallas_call | solution.py:347
  77.3 0.7 copy.9
  (1 shorter events, 0.0 us)
Async XLA Ops:
  0.0 3.3 %copy-start.2 = (s32[18432]{0:T(1024)S(1)}, s32[18432]{0:T(1024)}, u32[]{:S(2)}) copy-start(s32[18432]{0:T(1024)} %param.11) | copy-start | bytes 221188
  0.0 3.3 %copy-start.1 = (s32[18432]{0:T(1024)S(1)}, s32[18432]{0:T(1024)}, u32[]{:S(2)}) copy-start(s32[18432]{0:T(1024)} %param.10) | copy-start | bytes 221188
  0.0 3.3 %copy-start = (s32[18432]{0:T(1024)S(1)}, s32[18432]{0:T(1024)}, u32[]{:S(2)}) copy-start(s32[18432]{0:T(1024)} %param.9) | copy-start | bytes 221188
  0.0 3.3 %copy-start.3 = (f32[512]{0:T(512)S(1)}, f32[512]{0:T(512)}, u32[]{:S(2)}) copy-start(f32[512]{0:T(512)} %param.8) | copy-start | bytes 6148

commit v2 on v1

--- a/solution.py
+++ b/solution.py
@@ -16,7 +16,8 @@
 RANK = 512
 LAT = 576
 META = 64
-HALF_A = 72
+WIDE = LAT + META
+HALF_A = 80
 INV_SEGS = 7282
 
 
@@ -51,10 +52,33 @@
     return rolled[:, :SEGS_EACH]
 
 
+def encode(block):
+    latent, rotary = block[:, :RANK], block[:, RANK:]
+    codes, pieces = [], []
+    for piece in (latent, rotary):
+        top = jnp.max(jnp.abs(piece), axis=1, keepdims=True)
+        code = jnp.ceil(jnp.log2(jnp.maximum(top, 1e-30)) * 128.0 + 0.01)
+        codes.append(code)
+        pieces.append(piece * jnp.exp2(14.999 - code * (1.0 / 128.0)))
+    lane = last_axis_iota(block.shape[0], META)
+    pieces.append(jnp.where(lane < META // 2, codes[0], codes[1]))
+    coded = jnp.concatenate(pieces, axis=1)
+    return jnp.round(coded).astype(jnp.int32).astype(jnp.int16)
+
+
+def decode(coded):
+    block = coded.astype(jnp.int32).astype(jnp.float32)
+    pieces = []
+    for columns, place in ((slice(0, RANK), LAT), (slice(RANK, LAT), LAT + META // 2)):
+        scale = jnp.exp2(block[:, place : place + 1] * (1.0 / 128.0) - 14.999)
+        pieces.append(block[:, columns] * scale)
+    return jnp.concatenate(pieces, axis=1)
+
+
 def kernel(
     x_hbm, w_hbm, gain_ref, page_hbm, length_hbm, start_hbm, freq_ref, out_ref,
     x_buf, w_buf, page_buf, length_buf, start_buf,
-    part, opp_a, opp_b, from_left, from_right,
+    part, to_opposite, to_right, to_left, opposite, from_left, from_right,
     z_send0, z_send1, z_recv0, z_recv1, p_send0, p_send1, p_recv0, p_recv1,
     x_sem, w_sem, i_sem, ys, yr, zs, zr, ps, pr,
 ):
@@ -115,7 +139,9 @@
     def project(i):
         x_copies[i].wait()
         block = x_buf[i].reshape(2 * SEGS_EACH, x_buf.shape[-1])
-        result = jnp.dot(block, w_buf[...], preferred_element_type=jnp.float32)
+        result = lax.dot_general(
+            block, w_buf[...], (((1,), (1,)), ((), ())), preferred_element_type=jnp.float32
+        )
         part[i] = result.reshape(2, SEGS_EACH, LAT)
 
     def y_copy(src, dst, rho, kind, target):
@@ -132,27 +158,38 @@
     rows_b = pl.ds(HALF_A, SEGS_EACH - HALF_A)
     y_copies = [
         [
-            y_copy(part.at[0, rho, rows_a], opp_a.at[rho], rho, 0, right),
-            y_copy(part.at[0, rho, rows_b], opp_b.at[rho], rho, 1, left),
-            y_copy(part.at[1, rho, rows_b], from_left.at[rho, rows_b], rho, 2, right),
-            y_copy(part.at[2, rho, rows_a], from_right.at[rho, rows_a], rho, 3, left),
-            y_copy(part.at[1, rho, rows_a], from_left.at[rho, rows_a], rho, 4, right),
-            y_copy(part.at[2, rho, rows_b], from_right.at[rho, rows_b], rho, 5, left),
+            y_copy(to_opposite.at[rho, rows_a], opposite.at[rho, rows_a], rho, 0, right),
+            y_copy(to_opposite.at[rho, rows_b], opposite.at[rho, rows_b], rho, 1, left),
+            y_copy(to_right.at[rho, rows_b], from_left.at[rho, rows_b], rho, 2, right),
+            y_copy(to_left.at[rho, rows_a], from_right.at[rho, rows_a], rho, 3, left),
+            y_copy(to_right.at[rho, rows_a], from_left.at[rho, rows_a], rho, 4, right),
+            y_copy(to_left.at[rho, rows_b], from_right.at[rho, rows_b], rho, 5, left),
         ]
         for rho in range(2)
     ]
 
+    def send_opposite(rho):
+        to_opposite[rho] = encode(part[0, rho])
+        y_copies[rho][0].start()
+        y_copies[rho][1].start()
+
+    def send_right(rho):
+        to_right[rho, rows_b] = encode(part[1, rho, rows_b])
+        y_copies[rho][2].start()
+
+    def send_left(rho):
+        to_left[rho, rows_a] = encode(part[2, rho, rows_a])
+        y_copies[rho][3].start()
+
     w_copy.wait()
     project(0)
     pl.semaphore_wait(barrier, 2 + (NZ - 1) + (NQ - 1))
-    y_copies[0][0].start()
-    y_copies[0][1].start()
+    send_opposite(0)
     project(1)
-    y_copies[0][2].start()
+    send_right(0)
     project(2)
-    y_copies[0][3].start()
-    y_copies[1][0].start()
-    y_copies[1][1].start()
+    send_left(0)
+    send_opposite(1)
     project(3)
 
     for copy in index_copies:
@@ -193,16 +230,22 @@
 
     def add_and_pass(rho):
         y_copies[rho][0].wait_recv()
-        part[1, rho, rows_a] = part[1, rho, rows_a] + opp_a[rho]
+        to_right[rho, rows_a] = encode(part[1, rho, rows_a] + decode(opposite[rho, rows_a]))
         y_copies[rho][4].start()
         y_copies[rho][1].wait_recv()
-        part[2, rho, rows_b] = part[2, rho, rows_b] + opp_b[rho]
+        to_left[rho, rows_b] = encode(part[2, rho, rows_b] + decode(opposite[rho, rows_b]))
         y_copies[rho][5].start()
 
     add_and_pass(0)
-    y_copies[1][2].start()
-    y_copies[1][3].start()
-    add_and_pass(1)
+    send_right(1)
+    send_left(1)
+
+    def each_z(act):
+        def step(i, carry):
+            act(i + (i + NZ - z) // NZ)
+            return carry
+
+        lax.fori_loop(0, NZ - 1, step, 0)
 
     def z_copy(rho, other):
         return pltpu.make_async_remote_copy(
@@ -254,7 +297,7 @@
     def finish(rho):
         for kind in (2, 3, 4, 5):
             y_copies[rho][kind].wait_recv()
-        total = part[3, rho] + from_left[rho] + from_right[rho]
+        total = part[3, rho] + decode(from_left[rho]) + decode(from_right[rho])
         latent = total[:, :RANK]
         rotary = total[:, RANK:]
         mean_square = jnp.sum(latent * latent, axis=1, keepdims=True) * (1.0 / RANK)
@@ -271,10 +314,10 @@
         sent = jnp.dot(send_table, row.astype(jnp.bfloat16), preferred_element_type=jnp.float32)
         z_send[rho][...] = sent.astype(jnp.bfloat16).reshape(z_send[rho].shape)
         z_recv[rho][z] = z_send[rho][z]
-        each(NZ, z, lambda other: z_copy(rho, other).start())
+        each_z(lambda other: z_copy(rho, other).start())
 
     def turn(rho):
-        each(NZ, z, lambda other: z_arrival(rho, other).wait_recv())
+        each_z(lambda other: z_arrival(rho, other).wait_recv())
         arrived = z_recv[rho][...].reshape(slots, z_recv[rho].shape[-1])
         turned = jnp.dot(turn_table, arrived, preferred_element_type=jnp.float32)
         p_send[rho][...] = turned.astype(jnp.bfloat16).reshape(p_send[rho].shape)
@@ -282,11 +325,12 @@
         each(NQ, plane, lambda other: p_copy(rho, other).start())
 
     finish(0)
+    add_and_pass(1)
     finish(1)
     turn(0)
     turn(1)
     each(NQ, plane, lambda other: p_arrival(0, other).wait_recv())
-    landed = p_recv0[...].reshape(slots, LAT + META)
+    landed = p_recv0[...].reshape(slots, WIDE)
     place = as_row(landed[:, LAT : LAT + 1].astype(jnp.float32))
     page_ids = (first_axis_iota(SEGS_EACH, slots) + 1).astype(jnp.float32)
     take_table = jnp.where(page_ids == place, 1.0, 0.0).astype(jnp.bfloat16)
@@ -301,7 +345,7 @@
     for rho in range(2):
         for copy in y_copies[rho]:
             copy.wait_send()
-        each(NZ, z, lambda other: z_copy(rho, other).wait_send())
+        each_z(lambda other: z_copy(rho, other).wait_send())
         each(NQ, plane, lambda other: p_copy(rho, other).wait_send())
 
 
@@ -317,22 +361,24 @@
     n = SEGS_EACH
     scratch = [
         pltpu.VMEM((TP, 2, n, width), bf16),
-        pltpu.VMEM((width, LAT), bf16),
+        pltpu.VMEM((LAT, width), bf16),
         pltpu.VMEM((n, 128), jnp.int32),
         pltpu.VMEM((n, 128), jnp.int32),
         pltpu.VMEM((n, 128), jnp.int32),
         pltpu.VMEM((TP, 2, n, LAT), f32),
-        pltpu.VMEM((2, HALF_A, LAT), f32),
-        pltpu.VMEM((2, n - HALF_A, LAT), f32),
-        pltpu.VMEM((2, n, LAT), f32),
-        pltpu.VMEM((2, n, LAT), f32),
-        pltpu.VMEM((NZ, NQ * CAP, LAT + META), bf16),
+        pltpu.VMEM((2, n, WIDE), jnp.int16),
+        pltpu.VMEM((2, n, WIDE), jnp.int16),
+        pltpu.VMEM((2, n, WIDE), jnp.int16),
+        pltpu.VMEM((2, n, WIDE), jnp.int16),
+        pltpu.VMEM((2, n, WIDE), jnp.int16),
+        pltpu.VMEM((2, n, WIDE), jnp.int16),
+        pltpu.VMEM((NZ, NQ * CAP, WIDE), bf16),
         pltpu.VMEM((NZ, NQ * CAP, LAT), bf16),
-        pltpu.VMEM((NZ, NQ * CAP, LAT + META), bf16),
+        pltpu.VMEM((NZ, NQ * CAP, WIDE), bf16),
         pltpu.VMEM((NZ, NQ * CAP, LAT), bf16),
-        pltpu.VMEM((NQ, NZ * CAP, LAT + META), bf16),
+        pltpu.VMEM((NQ, NZ * CAP, WIDE), bf16),
         pltpu.VMEM((NQ, NZ * CAP, LAT), bf16),
-        pltpu.VMEM((NQ, NZ * CAP, LAT + META), bf16),
+        pltpu.VMEM((NQ, NZ * CAP, WIDE), bf16),
         pltpu.VMEM((NQ, NZ * CAP, LAT), bf16),
         dma((TP,)),
         dma(()),
@@ -359,7 +405,7 @@
         name="latent_rows",
     )(
         hidden_rows,
-        compress_weight,
+        compress_weight.T,
         latent_gain.reshape(1, RANK),
         segment_page.reshape(n, 128),
         segment_length.reshape(n, 128),

time: 78.2 us -> 69.7 us (0.89)
  Pallas kernels: 74 us -> 63.2 us
  local copies, waits for them, and re-layouts: 3.98 us -> 5.65 us
    pallas_call x1, Pallas kernels: 74 us -> 63.2 us  [shards(): pl.pallas_call(kernel, out_shape=jax.ShapeDtypeStruct((2, n, LAT), bf16),...]
    unnamed x10 -> x11, local copies, waits for them, and re-layouts: 3.98 us -> 5.65 us
where the time goes in v2:
time: 69.7 us; the launch traced here: 68.9 us
  Pallas kernels  63.2 us (91%)
  local copies, waits for them, and re-layouts  5.65 us (8%)
    pallas_call x1, Pallas kernels, shards(): pl.pallas_call(kernel, out_shape=jax.ShapeDtypeStruct((2, n, LAT), bf16),...  63.2 us
    unnamed x11, local copies, waits for them, and re-layouts  5.65 us

profile of v2, /device:TPU:1, one launch (start us, length us, event | category | flops | bytes accessed | tf_op | source)
XLA Modules:
  0.0 68.9 jit_solution(4777249087851542647)
XLA Ops:
  0.0 0.0 copy-start
  0.0 1.6 %copy-done = bf16[1792,576]{0,1:T(8,128)(2,1)S(1)} copy-done((bf16[1792,576]{0,1:T(8,128)(2,1)S(1)}, bf16[1792,576]{0,1:T(8,128)(2,1)}, u32[]{:S(2)}) %copy-start) | copy-done | bytes 2064408
  1.6 0.0 copy-start.1
  1.6 0.9 %copy-done.1 = s32[18432]{0:T(1024)S(1)} copy-done((s32[18432]{0:T(1024)S(1)}, s32[18432]{0:T(1024)}, u32[]{:S(2)}) %copy-start.1) | copy-done | bytes 73752
  2.5 0.0 copy-start.2
  2.5 0.9 %copy-done.2 = s32[18432]{0:T(1024)S(1)} copy-done((s32[18432]{0:T(1024)S(1)}, s32[18432]{0:T(1024)}, u32[]{:S(2)}) %copy-start.2) | copy-done | bytes 73752
  3.4 0.0 copy-start.3
  3.4 0.9 %copy-done.3 = s32[18432]{0:T(1024)S(1)} copy-done((s32[18432]{0:T(1024)S(1)}, s32[18432]{0:T(1024)}, u32[]{:S(2)}) %copy-start.3) | copy-done | bytes 73752
  4.3 0.0 copy-start.4
  4.3 0.7 copy-done.4
  4.9 63.2 %latent_rows.1 = bf16[2,144,576]{2,1,0:T(8,128)(2,1)S(1)} custom-call(bf16[8,144,1792]{2,1,0:T(8,128)(2,1)} %x_hbm.1, bf16[576,1792]{1,0:T(8,128)(2,1)S(1)} %bitcast.5, f32[1,512]{1,0:T(1,128)S(1)} %bitcast.9, s32[144,128]{1,0:T(8,128)S(1)} %bitcast.6, s32[144,128]{1,0:T(8,128)S(1)} %bitcast.7, s32[144,128]{1,0:T(8,128)S(1)} %bitcast.8, ...), custom_call_target="tpu_custom_call" | custom-call | flops 2378170368 | bytes 7000000 | tf_op jit(solution)/shard_map/latent_rows/pallas_call | solution.py:393
  68.2 0.7 %copy.8 = bf16[2,144,576]{2,1,0:T(8,128)(2,1)} copy(bf16[2,144,576]{2,1,0:T(8,128)(2,1)S(1)} %latent_rows.1) | data formatting | bytes 663552
  (1 shorter events, 0.0 us)
Async XLA Ops:
  0.0 1.6 %copy-start = (bf16[1792,576]{0,1:T(8,128)(2,1)S(1)}, bf16[1792,576]{0,1:T(8,128)(2,1)}, u32[]{:S(2)}) copy-start(bf16[1792,576]{0,1:T(8,128)(2,1)} %param.7) | copy-start | bytes 6193156
  1.6 0.9 %copy-start.1 = (s32[18432]{0:T(1024)S(1)}, s32[18432]{0:T(1024)}, u32[]{:S(2)}) copy-start(s32[18432]{0:T(1024)} %param.9) | copy-start | bytes 221188
  2.5 0.9 %copy-start.2 = (s32[18432]{0:T(1024)S(1)}, s32[18432]{0:T(1024)}, u32[]{:S(2)}) copy-start(s32[18432]{0:T(1024)} %param.10) | copy-start | bytes 221188
  3.4 0.9 %copy-start.3 = (s32[18432]{0:T(1024)S(1)}, s32[18432]{0:T(1024)}, u32[]{:S(2)}) copy-start(s32[18432]{0:T(1024)} %param.11) | copy-start | bytes 221188
  4.3 0.7 copy-start.4

commit v3 on v2

--- a/solution.py
+++ b/solution.py
@@ -17,7 +17,7 @@
 LAT = 576
 META = 64
 WIDE = LAT + META
-HALF_A = 80
+HALVES = 2
 INV_SEGS = 7282
 
 
@@ -76,9 +76,9 @@
 
 
 def kernel(
-    x_hbm, w_hbm, gain_ref, page_hbm, length_hbm, start_hbm, freq_ref, out_ref,
-    x_buf, w_buf, page_buf, length_buf, start_buf,
-    part, to_opposite, to_right, to_left, opposite, from_left, from_right,
+    x_hbm, w_hbm, gain_hbm, page_hbm, length_hbm, start_hbm, freq_hbm, out_ref,
+    x_buf, w_buf, gain_buf, page_buf, length_buf, start_buf, freq_buf,
+    part, coded, arrived_rows,
     z_send0, z_send1, z_recv0, z_recv1, p_send0, p_send1, p_recv0, p_recv1,
     x_sem, w_sem, i_sem, ys, yr, zs, zr, ps, pr,
 ):
@@ -111,14 +111,20 @@
     index_copies = [
         pltpu.make_async_copy(src, dst, i_sem.at[i])
         for i, (src, dst) in enumerate(
-            ((page_hbm, page_buf), (length_hbm, length_buf), (start_hbm, start_buf))
+            (
+                (page_hbm, page_buf),
+                (length_hbm, length_buf),
+                (start_hbm, start_buf),
+                (gain_hbm, gain_buf),
+                (freq_hbm, freq_buf),
+            )
         )
     ]
     for copy in index_copies:
         copy.start()
 
     barrier = pltpu.get_barrier_semaphore()
-    for neighbour in (left, right):
+    for neighbour in targets[:3]:
         pl.semaphore_signal(barrier, inc=1, device_id=(dec, neighbour), device_id_type=MESH)
 
     def greet_z(i, carry):
@@ -136,61 +142,40 @@
     lax.fori_loop(1, NZ, greet_z, 0)
     lax.fori_loop(1, NQ, greet_p, 0)
 
-    def project(i):
-        x_copies[i].wait()
-        block = x_buf[i].reshape(2 * SEGS_EACH, x_buf.shape[-1])
+    def project(rho, i):
         result = lax.dot_general(
-            block, w_buf[...], (((1,), (1,)), ((), ())), preferred_element_type=jnp.float32
-        )
-        part[i] = result.reshape(2, SEGS_EACH, LAT)
-
-    def y_copy(src, dst, rho, kind, target):
-        return pltpu.make_async_remote_copy(
-            src_ref=src,
-            dst_ref=dst,
-            send_sem=ys.at[rho, kind],
-            recv_sem=yr.at[rho, kind],
-            device_id=(dec, target),
-            device_id_type=MESH,
-        )
-
-    rows_a = pl.ds(0, HALF_A)
-    rows_b = pl.ds(HALF_A, SEGS_EACH - HALF_A)
+            x_buf[i, rho], w_buf[...], (((1,), (1,)), ((), ())), preferred_element_type=jnp.float32
+        )
+        if i == TP - 1:
+            part[rho] = result
+        else:
+            coded[rho, i] = encode(result)
+
     y_copies = [
         [
-            y_copy(to_opposite.at[rho, rows_a], opposite.at[rho, rows_a], rho, 0, right),
-            y_copy(to_opposite.at[rho, rows_b], opposite.at[rho, rows_b], rho, 1, left),
-            y_copy(to_right.at[rho, rows_b], from_left.at[rho, rows_b], rho, 2, right),
-            y_copy(to_left.at[rho, rows_a], from_right.at[rho, rows_a], rho, 3, left),
-            y_copy(to_right.at[rho, rows_a], from_left.at[rho, rows_a], rho, 4, right),
-            y_copy(to_left.at[rho, rows_b], from_right.at[rho, rows_b], rho, 5, left),
+            pltpu.make_async_remote_copy(
+                src_ref=coded.at[rho, i],
+                dst_ref=arrived_rows.at[rho, i],
+                send_sem=ys.at[rho, i],
+                recv_sem=yr.at[rho, i],
+                device_id=(dec, targets[i]),
+                device_id_type=MESH,
+            )
+            for i in range(TP - 1)
         ]
         for rho in range(2)
     ]
 
-    def send_opposite(rho):
-        to_opposite[rho] = encode(part[0, rho])
-        y_copies[rho][0].start()
-        y_copies[rho][1].start()
-
-    def send_right(rho):
-        to_right[rho, rows_b] = encode(part[1, rho, rows_b])
-        y_copies[rho][2].start()
-
-    def send_left(rho):
-        to_left[rho, rows_a] = encode(part[2, rho, rows_a])
-        y_copies[rho][3].start()
-
     w_copy.wait()
-    project(0)
-    pl.semaphore_wait(barrier, 2 + (NZ - 1) + (NQ - 1))
-    send_opposite(0)
-    project(1)
-    send_right(0)
-    project(2)
-    send_left(0)
-    send_opposite(1)
-    project(3)
+    x_copies[0].wait()
+    project(0, 0)
+    pl.semaphore_wait(barrier, (TP - 1) + (NZ - 1) + (NQ - 1))
+    y_copies[0][0].start()
+    for i in range(1, TP):
+        x_copies[i].wait()
+        project(0, i)
+        if i < TP - 1:
+            y_copies[0][i].start()
 
     for copy in index_copies:
         copy.wait()
@@ -217,28 +202,22 @@
     ).astype(jnp.bfloat16)
     meta = jnp.broadcast_to(place_col + 1.0, (SEGS_EACH, META))
 
-    out_slot = first_axis_iota(slots, slots)
-    in_slot = last_axis_iota(slots, slots)
-    wanted = ((out_slot >> 1) & (NZ - 1)) * (NQ * CAP) + (out_slot >> 5) * CAP + (out_slot & 1)
+    half_slots = slots // HALVES
+    out_slot = first_axis_iota(half_slots, half_slots)
+    in_slot = last_axis_iota(half_slots, half_slots)
+    z_of_slot = (out_slot // CAP) % (NZ // HALVES)
+    plane_of_slot = out_slot // (CAP * NZ // HALVES)
+    wanted = z_of_slot * (NQ * CAP) + plane_of_slot * CAP + out_slot % CAP
     turn_table = jnp.where(wanted == in_slot, 1.0, 0.0).astype(jnp.bfloat16)
 
     angles = []
     for rho in range(2):
         position = start_col + (2 * tp + rho).astype(jnp.float32)
-        phase = position * freq_ref[...]
+        phase = position * freq_buf[...]
         angles.append((jnp.cos(phase), jnp.sin(phase)))
 
-    def add_and_pass(rho):
-        y_copies[rho][0].wait_recv()
-        to_right[rho, rows_a] = encode(part[1, rho, rows_a] + decode(opposite[rho, rows_a]))
-        y_copies[rho][4].start()
-        y_copies[rho][1].wait_recv()
-        to_left[rho, rows_b] = encode(part[2, rho, rows_b] + decode(opposite[rho, rows_b]))
-        y_copies[rho][5].start()
-
-    add_and_pass(0)
-    send_right(1)
-    send_left(1)
+    for i in range(TP):
+        project(1, i)
 
     def each_z(act):
         def step(i, carry):
@@ -267,22 +246,22 @@
             device_id_type=MESH,
         )
 
-    def p_copy(rho, other):
+    def p_copy(rho, half, other):
         return pltpu.make_async_remote_copy(
-            src_ref=p_send[rho].at[other],
-            dst_ref=p_recv[rho].at[plane],
-            send_sem=ps.at[rho, other],
-            recv_sem=pr.at[rho, plane],
+            src_ref=p_send[rho].at[half, other],
+            dst_ref=p_recv[rho].at[half, plane],
+            send_sem=ps.at[rho, half, other],
+            recv_sem=pr.at[rho, half, plane],
             device_id=(p_device(other), tp),
             device_id_type=MESH,
         )
 
-    def p_arrival(rho, other):
+    def p_arrival(rho, half, other):
         return pltpu.make_async_remote_copy(
-            src_ref=p_send[rho].at[other],
-            dst_ref=p_recv[rho].at[other],
-            send_sem=ps.at[rho, other],
-            recv_sem=pr.at[rho, other],
+            src_ref=p_send[rho].at[half, other],
+            dst_ref=p_recv[rho].at[half, other],
+            send_sem=ps.at[rho, half, other],
+            recv_sem=pr.at[rho, half, other],
             device_id=(p_device(other), tp),
             device_id_type=MESH,
         )
@@ -295,13 +274,14 @@
         lax.fori_loop(1, count, step, 0)
 
     def finish(rho):
-        for kind in (2, 3, 4, 5):
-            y_copies[rho][kind].wait_recv()
-        total = part[3, rho] + decode(from_left[rho]) + decode(from_right[rho])
+        total = part[rho]
+        for i in range(TP - 1):
+            y_copies[rho][i].wait_recv()
+            total = total + decode(arrived_rows[rho, i])
         latent = total[:, :RANK]
         rotary = total[:, RANK:]
         mean_square = jnp.sum(latent * latent, axis=1, keepdims=True) * (1.0 / RANK)
-        latent = latent / jnp.sqrt(mean_square + 1e-06) * gain_ref[...]
+        latent = latent / jnp.sqrt(mean_square + 1e-06) * gain_buf[...]
         half = (LAT - RANK) // 2
         front, back = rotary[:, :half], rotary[:, half:]
         cosine, sine = angles[rho]
@@ -316,37 +296,56 @@
         z_recv[rho][z] = z_send[rho][z]
         each_z(lambda other: z_copy(rho, other).start())
 
-    def turn(rho):
-        each_z(lambda other: z_arrival(rho, other).wait_recv())
-        arrived = z_recv[rho][...].reshape(slots, z_recv[rho].shape[-1])
-        turned = jnp.dot(turn_table, arrived, preferred_element_type=jnp.float32)
-        p_send[rho][...] = turned.astype(jnp.bfloat16).reshape(p_send[rho].shape)
-        p_recv[rho][plane] = p_send[rho][plane]
-        each(NQ, plane, lambda other: p_copy(rho, other).start())
+    def turn(rho, half):
+        def wait_for(i, carry):
+            source = half * (NZ // HALVES) + i
+
+            @pl.when(source != z)
+            def _():
+                z_arrival(rho, source).wait_recv()
+
+            return carry
+
+        lax.fori_loop(0, NZ // HALVES, wait_for, 0)
+        wide = z_recv[rho].shape[-1]
+        arrived = z_recv[rho][half * (NZ // HALVES) : (half + 1) * (NZ // HALVES)]
+        turned = jnp.dot(
+            turn_table, arrived.reshape(slots // HALVES, wide), preferred_element_type=jnp.float32
+        )
+        p_send[rho][half] = turned.astype(jnp.bfloat16).reshape(p_send[rho].shape[1:])
+        p_recv[rho][half, plane] = p_send[rho][half, plane]
+        each(NQ, plane, lambda other: p_copy(rho, half, other).start())
+
+    def land(rho, take_table):
+        for half in range(HALVES):
+            each(NQ, plane, lambda other: p_arrival(rho, half, other).wait_recv())
+        landed = p_recv[rho][...].reshape(slots, p_recv[rho].shape[-1])
+        if rho == 0:
+            place = as_row(landed[:, LAT : LAT + 1].astype(jnp.float32))
+            page_ids = (first_axis_iota(SEGS_EACH, slots) + 1).astype(jnp.float32)
+            take_table = jnp.where(page_ids == place, 1.0, 0.0).astype(jnp.bfloat16)
+        out_ref[rho] = jnp.dot(
+            take_table, landed[:, :LAT], preferred_element_type=jnp.float32
+        ).astype(jnp.bfloat16)
+        return take_table
 
     finish(0)
-    add_and_pass(1)
+    for i in range(TP - 1):
+        y_copies[1][i].start()
     finish(1)
-    turn(0)
-    turn(1)
-    each(NQ, plane, lambda other: p_arrival(0, other).wait_recv())
-    landed = p_recv0[...].reshape(slots, WIDE)
-    place = as_row(landed[:, LAT : LAT + 1].astype(jnp.float32))
-    page_ids = (first_axis_iota(SEGS_EACH, slots) + 1).astype(jnp.float32)
-    take_table = jnp.where(page_ids == place, 1.0, 0.0).astype(jnp.bfloat16)
-    out_ref[0] = jnp.dot(
-        take_table, landed[:, :LAT], preferred_element_type=jnp.float32
-    ).astype(jnp.bfloat16)
-    each(NQ, plane, lambda other: p_arrival(1, other).wait_recv())
-    out_ref[1] = jnp.dot(
-        take_table, p_recv1[...].reshape(slots, LAT), preferred_element_type=jnp.float32
-    ).astype(jnp.bfloat16)
+    turn(0, 0)
+    turn(0, 1)
+    turn(1, 0)
+    take_table = land(0, None)
+    turn(1, 1)
+    land(1, take_table)
 
     for rho in range(2):
         for copy in y_copies[rho]:
             copy.wait_send()
         each_z(lambda other: z_copy(rho, other).wait_send())
-        each(NQ, plane, lambda other: p_copy(rho, other).wait_send())
+        for half in range(HALVES):
+            each(NQ, plane, lambda other: p_copy(rho, half, other).wait_send())
 
 
 def shards(hidden_rows, compress_weight, latent_gain, segment_page, segment_length, segment_start):
@@ -359,45 +358,44 @@
     dma = pltpu.SemaphoreType.DMA
     bf16, f32 = jnp.bfloat16, jnp.float32
     n = SEGS_EACH
+    slot_rows = NZ // HALVES * CAP
     scratch = [
         pltpu.VMEM((TP, 2, n, width), bf16),
         pltpu.VMEM((LAT, width), bf16),
+        pltpu.VMEM((1, RANK), f32),
         pltpu.VMEM((n, 128), jnp.int32),
         pltpu.VMEM((n, 128), jnp.int32),
         pltpu.VMEM((n, 128), jnp.int32),
-        pltpu.VMEM((TP, 2, n, LAT), f32),
-        pltpu.VMEM((2, n, WIDE), jnp.int16),
-        pltpu.VMEM((2, n, WIDE), jnp.int16),
-        pltpu.VMEM((2, n, WIDE), jnp.int16),
-        pltpu.VMEM((2, n, WIDE), jnp.int16),
-        pltpu.VMEM((2, n, WIDE), jnp.int16),
-        pltpu.VMEM((2, n, WIDE), jnp.int16),
+        pltpu.VMEM((1, half), f32),
+        pltpu.VMEM((2, n, LAT), f32),
+        pltpu.VMEM((2, TP - 1, n, WIDE), jnp.int16),
+        pltpu.VMEM((2, TP - 1, n, WIDE), jnp.int16),
         pltpu.VMEM((NZ, NQ * CAP, WIDE), bf16),
         pltpu.VMEM((NZ, NQ * CAP, LAT), bf16),
         pltpu.VMEM((NZ, NQ * CAP, WIDE), bf16),
         pltpu.VMEM((NZ, NQ * CAP, LAT), bf16),
-        pltpu.VMEM((NQ, NZ * CAP, WIDE), bf16),
-        pltpu.VMEM((NQ, NZ * CAP, LAT), bf16),
-        pltpu.VMEM((NQ, NZ * CAP, WIDE), bf16),
-        pltpu.VMEM((NQ, NZ * CAP, LAT), bf16),
+        pltpu.VMEM((HALVES, NQ, slot_rows, WIDE), bf16),
+        pltpu.VMEM((HALVES, NQ, slot_rows, LAT), bf16),
+        pltpu.VMEM((HALVES, NQ, slot_rows, WIDE), bf16),
+        pltpu.VMEM((HALVES, NQ, slot_rows, LAT), bf16),
         dma((TP,)),
         dma(()),
-        dma((3,)),
-        dma((2, 6)),
-        dma((2, 6)),
+        dma((5,)),
+        dma((2, TP - 1)),
+        dma((2, TP - 1)),
         dma((2, NZ)),
         dma((2, NZ)),
-        dma((2, NQ)),
-        dma((2, NQ)),
+        dma((2, HALVES, NQ)),
+        dma((2, HALVES, NQ)),
     ]
     return pl.pallas_call(
         kernel,
         out_shape=jax.ShapeDtypeStruct((2, n, LAT), bf16),
-        in_specs=[any_spec, any_spec, vmem_spec, any_spec, any_spec, any_spec, vmem_spec],
+        in_specs=[any_spec] * 7,
         out_specs=vmem_spec,
         scratch_shapes=scratch,
         compiler_params=pltpu.CompilerParams(
-            collective_id=0, has_side_effects=True, vmem_limit_bytes=50 * 1024 * 1024
+            collective_id=0, has_side_effects=True, vmem_limit_bytes=60 * 1024 * 1024
         ),
         cost_estimate=pl.CostEstimate(
             flops=2 * 8 * n * width * LAT, bytes_accessed=7_000_000, transcendentals=0

time: 69.7 us -> 66.1 us (0.948)
  local copies, waits for them, and re-layouts: 5.65 us -> 1.76 us
    unnamed x11 -> x1, local copies, waits for them, and re-layouts: 5.65 us -> 1.76 us
where the time goes in v3:
time: 66.1 us; the launch traced here: 65.1 us
  Pallas kernels  62.8 us (95%)
  local copies, waits for them, and re-layouts  1.76 us (3%)
    pallas_call x1, Pallas kernels, shards(): pl.pallas_call(kernel, out_shape=jax.ShapeDtypeStruct((2, n, LAT), bf16),...  62.8 us
    unnamed x1, local copies, waits for them, and re-layouts  1.76 us

profile of v3, /device:TPU:1, one launch (start us, length us, event | category | flops | bytes accessed | tf_op | source)
XLA Modules:
  0.0 65.1 jit_solution(7115981588016993822)
XLA Ops:
  0.0 0.5 negate_power_fusion.freq_hbm
  0.5 62.8 %latent_rows.1 = bf16[2,144,576]{2,1,0:T(8,128)(2,1)} custom-call(bf16[8,144,1792]{2,1,0:T(8,128)(2,1)} %x_hbm.1, bf16[576,1792]{1,0:T(8,128)(2,1)} %bitcast.5, f32[1,512]{1,0:T(1,128)} %bitcast.9, s32[144,128]{1,0:T(8,128)} %bitcast.6, s32[144,128]{1,0:T(8,128)} %bitcast.7, s32[144,128]{1,0:T(8,128)} %bitcast.8, f32[1,32]{1,0:T(1,128)} %negate_power_fusion.freq_hbm), custom_call_target="tpu_custom_call" | custom-call | flops 2378170368 | bytes 7000000 | tf_op jit(solution)/shard_map/latent_rows/pallas_call | solution.py:391
  63.3 1.8 %copy.8 = bf16[2,144,576]{2,1,0:T(8,128)(2,1)} copy(bf16[2,144,576]{2,1,0:T(8,128)(2,1)} %latent_rows.1) | data formatting | bytes 663552

commit v4 on v2

--- a/solution.py
+++ b/solution.py
@@ -2,6 +2,7 @@
 
 import jax
 import jax.numpy as jnp
+import numpy as np
 from jax import lax
 from jax.experimental import pallas as pl
 from jax.experimental.pallas import tpu as pltpu
@@ -76,8 +77,8 @@
 
 
 def kernel(
-    x_hbm, w_hbm, gain_ref, page_hbm, length_hbm, start_hbm, freq_ref, out_ref,
-    x_buf, w_buf, page_buf, length_buf, start_buf,
+    x_hbm, w_hbm, gain_hbm, page_hbm, length_hbm, start_hbm, freq_hbm, out_ref,
+    x_buf, w_buf, gain_buf, page_buf, length_buf, start_buf, freq_buf,
     part, to_opposite, to_right, to_left, opposite, from_left, from_right,
     z_send0, z_send1, z_recv0, z_recv1, p_send0, p_send1, p_recv0, p_recv1,
     x_sem, w_sem, i_sem, ys, yr, zs, zr, ps, pr,
@@ -111,7 +112,13 @@
     index_copies = [
         pltpu.make_async_copy(src, dst, i_sem.at[i])
         for i, (src, dst) in enumerate(
-            ((page_hbm, page_buf), (length_hbm, length_buf), (start_hbm, start_buf))
+            (
+                (page_hbm, page_buf),
+                (length_hbm, length_buf),
+                (start_hbm, start_buf),
+                (gain_hbm, gain_buf),
+                (freq_hbm, freq_buf),
+            )
         )
     ]
     for copy in index_copies:
@@ -136,13 +143,13 @@
     lax.fori_loop(1, NZ, greet_z, 0)
     lax.fori_loop(1, NQ, greet_p, 0)
 
-    def project(i):
-        x_copies[i].wait()
-        block = x_buf[i].reshape(2 * SEGS_EACH, x_buf.shape[-1])
-        result = lax.dot_general(
-            block, w_buf[...], (((1,), (1,)), ((), ())), preferred_element_type=jnp.float32
-        )
-        part[i] = result.reshape(2, SEGS_EACH, LAT)
+    rows_a = pl.ds(0, HALF_A)
+    rows_b = pl.ds(HALF_A, SEGS_EACH - HALF_A)
+
+    def project(rho, i):
+        return lax.dot_general(
+            x_buf[i, rho], w_buf[...], (((1,), (1,)), ((), ())), preferred_element_type=jnp.float32
+        )
 
     def y_copy(src, dst, rho, kind, target):
         return pltpu.make_async_remote_copy(
@@ -154,8 +161,6 @@
             device_id_type=MESH,
         )
 
-    rows_a = pl.ds(0, HALF_A)
-    rows_b = pl.ds(HALF_A, SEGS_EACH - HALF_A)
     y_copies = [
         [
             y_copy(to_opposite.at[rho, rows_a], opposite.at[rho, rows_a], rho, 0, right),
@@ -168,29 +173,41 @@
         for rho in range(2)
     ]
 
-    def send_opposite(rho):
-        to_opposite[rho] = encode(part[0, rho])
-        y_copies[rho][0].start()
-        y_copies[rho][1].start()
-
-    def send_right(rho):
-        to_right[rho, rows_b] = encode(part[1, rho, rows_b])
-        y_copies[rho][2].start()
-
-    def send_left(rho):
-        to_left[rho, rows_a] = encode(part[2, rho, rows_a])
-        y_copies[rho][3].start()
+    def project_right(rho):
+        result = project(rho, 1)
+        to_right[rho, rows_b] = encode(result[HALF_A:])
+        part[rho, 1, rows_a] = result[:HALF_A]
+
+    def project_left(rho):
+        result = project(rho, 2)
+        to_left[rho, rows_a] = encode(result[:HALF_A])
+        part[rho, 2, rows_b] = result[HALF_A:]
+
+    def start(rho, *kinds):
+        for kind in kinds:
+            y_copies[rho][kind].start()
+
+    def add_and_pass(rho):
+        y_copies[rho][0].wait_recv()
+        to_right[rho, rows_a] = encode(part[rho, 1, rows_a] + decode(opposite[rho, rows_a]))
+        start(rho, 4)
+        y_copies[rho][1].wait_recv()
+        to_left[rho, rows_b] = encode(part[rho, 2, rows_b] + decode(opposite[rho, rows_b]))
+        start(rho, 5)
 
     w_copy.wait()
-    project(0)
+    x_copies[0].wait()
+    to_opposite[0] = encode(project(0, 0))
     pl.semaphore_wait(barrier, 2 + (NZ - 1) + (NQ - 1))
-    send_opposite(0)
-    project(1)
-    send_right(0)
-    project(2)
-    send_left(0)
-    send_opposite(1)
-    project(3)
+    start(0, 0, 1)
+    x_copies[1].wait()
+    project_right(0)
+    start(0, 2)
+    x_copies[2].wait()
+    project_left(0)
+    start(0, 3)
+    x_copies[3].wait()
+    part[0, 0] = project(0, 3)
 
     for copy in index_copies:
         copy.wait()
@@ -210,35 +227,35 @@
     ).astype(jnp.int32)
     owner_plane = (owner_row >> 5) * 2 + (owner_row & 1)
     owner_z = (owner_row >> 1) & (NZ - 1)
-    slot_row = owner_z * (NQ * CAP) + owner_plane * CAP + earlier_row
     slots = NZ * NQ * CAP
-    send_table = jnp.where(
-        first_axis_iota(slots, SEGS_EACH) == slot_row, 1.0, 0.0
-    ).astype(jnp.bfloat16)
+    slot_rows = (
+        owner_z * (NQ * CAP) + owner_plane * CAP + earlier_row,
+        owner_plane * (NZ * CAP) + owner_z * CAP + earlier_row,
+    )
+    send_tables = [
+        jnp.where(first_axis_iota(slots, SEGS_EACH) == row, 1.0, 0.0).astype(jnp.bfloat16)
+        for row in slot_rows
+    ]
     meta = jnp.broadcast_to(place_col + 1.0, (SEGS_EACH, META))
 
-    out_slot = first_axis_iota(slots, slots)
-    in_slot = last_axis_iota(slots, slots)
-    wanted = ((out_slot >> 1) & (NZ - 1)) * (NQ * CAP) + (out_slot >> 5) * CAP + (out_slot & 1)
-    turn_table = jnp.where(wanted == in_slot, 1.0, 0.0).astype(jnp.bfloat16)
+    by_plane = first_axis_iota(slots, slots)
+    by_z = last_axis_iota(slots, slots)
+    wanted = ((by_plane // CAP) % NZ) * (NQ * CAP) + by_plane // (CAP * NZ) * CAP + by_plane % CAP
+    to_plane_order = jnp.where(wanted == by_z, 1.0, 0.0).astype(jnp.bfloat16)
+    by_z, by_plane = first_axis_iota(slots, slots), last_axis_iota(slots, slots)
+    wanted = ((by_z // CAP) % NQ) * (NZ * CAP) + by_z // (CAP * NQ) * CAP + by_z % CAP
+    to_z_order = jnp.where(wanted == by_plane, 1.0, 0.0).astype(jnp.bfloat16)
 
     angles = []
     for rho in range(2):
         position = start_col + (2 * tp + rho).astype(jnp.float32)
-        phase = position * freq_ref[...]
+        phase = position * freq_buf[...]
         angles.append((jnp.cos(phase), jnp.sin(phase)))
 
-    def add_and_pass(rho):
-        y_copies[rho][0].wait_recv()
-        to_right[rho, rows_a] = encode(part[1, rho, rows_a] + decode(opposite[rho, rows_a]))
-        y_copies[rho][4].start()
-        y_copies[rho][1].wait_recv()
-        to_left[rho, rows_b] = encode(part[2, rho, rows_b] + decode(opposite[rho, rows_b]))
-        y_copies[rho][5].start()
-
     add_and_pass(0)
-    send_right(1)
-    send_left(1)
+    to_opposite[1] = encode(project(1, 0))
+    project_right(1)
+    project_left(1)
 
     def each_z(act):
         def step(i, carry):
@@ -297,11 +314,11 @@
     def finish(rho):
         for kind in (2, 3, 4, 5):
             y_copies[rho][kind].wait_recv()
-        total = part[3, rho] + decode(from_left[rho]) + decode(from_right[rho])
+        total = part[rho, 0] + decode(from_left[rho]) + decode(from_right[rho])
         latent = total[:, :RANK]
         rotary = total[:, RANK:]
         mean_square = jnp.sum(latent * latent, axis=1, keepdims=True) * (1.0 / RANK)
-        latent = latent / jnp.sqrt(mean_square + 1e-06) * gain_ref[...]
+        latent = latent / jnp.sqrt(mean_square + 1e-06) * gain_buf[...]
         half = (LAT - RANK) // 2
         front, back = rotary[:, :half], rotary[:, half:]
         cosine, sine = angles[rho]
@@ -311,36 +328,45 @@
         row = jnp.where(alive, row, 0.0)
         if rho == 0:
             row = jnp.concatenate([row, meta], axis=1)
-        sent = jnp.dot(send_table, row.astype(jnp.bfloat16), preferred_element_type=jnp.float32)
-        z_send[rho][...] = sent.astype(jnp.bfloat16).reshape(z_send[rho].shape)
+        return jnp.dot(
+            send_tables[rho], row.astype(jnp.bfloat16), preferred_element_type=jnp.float32
+        ).astype(jnp.bfloat16)
+
+    def send_z(rho, rows):
+        z_send[rho][...] = rows.reshape(z_send[rho].shape)
         z_recv[rho][z] = z_send[rho][z]
         each_z(lambda other: z_copy(rho, other).start())
 
-    def turn(rho):
-        each_z(lambda other: z_arrival(rho, other).wait_recv())
-        arrived = z_recv[rho][...].reshape(slots, z_recv[rho].shape[-1])
-        turned = jnp.dot(turn_table, arrived, preferred_element_type=jnp.float32)
-        p_send[rho][...] = turned.astype(jnp.bfloat16).reshape(p_send[rho].shape)
+    def send_p(rho, rows):
+        p_send[rho][...] = rows.reshape(p_send[rho].shape)
         p_recv[rho][plane] = p_send[rho][plane]
         each(NQ, plane, lambda other: p_copy(rho, other).start())
 
-    finish(0)
+    def arrived_z(rho):
+        each_z(lambda other: z_arrival(rho, other).wait_recv())
+        return z_recv[rho][...].reshape(slots, z_recv[rho].shape[-1])
+
+    def arrived_p(rho):
+        each(NQ, plane, lambda other: p_arrival(rho, other).wait_recv())
+        return p_recv[rho][...].reshape(slots, p_recv[rho].shape[-1])
+
+    def reorder(table, rows):
+        return jnp.dot(table, rows, preferred_element_type=jnp.float32).astype(jnp.bfloat16)
+
+    send_z(0, finish(0))
+    start(1, 0, 1, 2, 3)
+    part[1, 0] = project(1, 3)
     add_and_pass(1)
-    finish(1)
-    turn(0)
-    turn(1)
-    each(NQ, plane, lambda other: p_arrival(0, other).wait_recv())
-    landed = p_recv0[...].reshape(slots, WIDE)
+    send_p(1, finish(1))
+    send_z(1, reorder(to_z_order, arrived_p(1)))
+    send_p(0, reorder(to_plane_order, arrived_z(0)))
+    landed = arrived_p(0)
     place = as_row(landed[:, LAT : LAT + 1].astype(jnp.float32))
     page_ids = (first_axis_iota(SEGS_EACH, slots) + 1).astype(jnp.float32)
     take_table = jnp.where(page_ids == place, 1.0, 0.0).astype(jnp.bfloat16)
-    out_ref[0] = jnp.dot(
-        take_table, landed[:, :LAT], preferred_element_type=jnp.float32
-    ).astype(jnp.bfloat16)
-    each(NQ, plane, lambda other: p_arrival(1, other).wait_recv())
-    out_ref[1] = jnp.dot(
-        take_table, p_recv1[...].reshape(slots, LAT), preferred_element_type=jnp.float32
-    ).astype(jnp.bfloat16)
+    out_ref[0] = reorder(take_table, landed[:, :LAT])
+    take_table = reorder(take_table, to_plane_order)
+    out_ref[1] = reorder(take_table, arrived_z(1))
 
     for rho in range(2):
         for copy in y_copies[rho]:
@@ -351,8 +377,8 @@
 
 def shards(hidden_rows, compress_weight, latent_gain, segment_page, segment_length, segment_start):
     half = (LAT - RANK) // 2
-    exponent = jnp.arange(half, dtype=jnp.float32) * (2.0 / (LAT - RANK))
-    frequency = jnp.power(jnp.float32(10000.0), -exponent).reshape(1, half)
+    exponent = np.arange(half, dtype=np.float64) * (2.0 / (LAT - RANK))
+    frequency = jnp.asarray(np.power(10000.0, -exponent).reshape(1, half).astype(np.float32))
     width = hidden_rows.shape[-1]
     any_spec = pl.BlockSpec(memory_space=pltpu.HBM)
     vmem_spec = pl.BlockSpec(memory_space=pltpu.VMEM)
@@ -362,10 +388,12 @@
     scratch = [
         pltpu.VMEM((TP, 2, n, width), bf16),
         pltpu.VMEM((LAT, width), bf16),
+        pltpu.VMEM((1, RANK), f32),
         pltpu.VMEM((n, 128), jnp.int32),
         pltpu.VMEM((n, 128), jnp.int32),
         pltpu.VMEM((n, 128), jnp.int32),
-        pltpu.VMEM((TP, 2, n, LAT), f32),
+        pltpu.VMEM((1, half), f32),
+        pltpu.VMEM((2, TP - 1, n, LAT), f32),
         pltpu.VMEM((2, n, WIDE), jnp.int16),
         pltpu.VMEM((2, n, WIDE), jnp.int16),
         pltpu.VMEM((2, n, WIDE), jnp.int16),
@@ -382,7 +410,7 @@
         pltpu.VMEM((NQ, NZ * CAP, LAT), bf16),
         dma((TP,)),
         dma(()),
-        dma((3,)),
+        dma((5,)),
         dma((2, 6)),
         dma((2, 6)),
         dma((2, NZ)),
@@ -393,11 +421,11 @@
     return pl.pallas_call(
         kernel,
         out_shape=jax.ShapeDtypeStruct((2, n, LAT), bf16),
-        in_specs=[any_spec, any_spec, vmem_spec, any_spec, any_spec, any_spec, vmem_spec],
+        in_specs=[any_spec] * 7,
         out_specs=vmem_spec,
         scratch_shapes=scratch,
         compiler_params=pltpu.CompilerParams(
-            collective_id=0, has_side_effects=True, vmem_limit_bytes=50 * 1024 * 1024
+            collective_id=0, has_side_effects=True, vmem_limit_bytes=60 * 1024 * 1024
         ),
         cost_estimate=pl.CostEstimate(
             flops=2 * 8 * n * width * LAT, bytes_accessed=7_000_000, transcendentals=0

time: 69.7 us -> 60.1 us (0.86)
  the two profiles are of different devices: /device:TPU:1 before, /device:TPU:169 now
where the time goes in v4:
time: 60.1 us; the launch traced here: 60 us
  Pallas kernels  58.2 us (97%)
  local copies, waits for them, and re-layouts  1.76 us (3%)
    pallas_call x1, Pallas kernels, shards(): pl.pallas_call(kernel, out_shape=jax.ShapeDtypeStruct((2, n, LAT), bf16),...  58.2 us
    unnamed x1, local copies, waits for them, and re-layouts  1.76 us

profile of v4, /device:TPU:169, one launch (start us, length us, event | category | flops | bytes accessed | tf_op | source)
XLA Modules:
  0.0 60.0 jit_solution(10076683615296627026)
XLA Ops:
  0.0 58.2 %latent_rows.1 = bf16[2,144,576]{2,1,0:T(8,128)(2,1)} custom-call(bf16[8,144,1792]{2,1,0:T(8,128)(2,1)} %x_hbm.1, bf16[576,1792]{1,0:T(8,128)(2,1)} %bitcast.5, f32[1,512]{1,0:T(1,128)} %bitcast.9, s32[144,128]{1,0:T(8,128)} %bitcast.6, s32[144,128]{1,0:T(8,128)} %bitcast.7, s32[144,128]{1,0:T(8,128)} %bitcast.8, f32[1,32]{1,0:T(1,128)} %constant.2.clone.freq_hbm), custom_call_target="tpu_custom_call" | custom-call | flops 2378170368 | bytes 7000000 | tf_op jit(solution)/shard_map/latent_rows/pallas_call | solution.py:421
  58.2 1.8 %copy.9 = bf16[2,144,576]{2,1,0:T(8,128)(2,1)} copy(bf16[2,144,576]{2,1,0:T(8,128)(2,1)} %latent_rows.1) | data formatting | bytes 663552

commit v5 on v4

--- a/solution.py
+++ b/solution.py
@@ -16,8 +16,9 @@
 SEGS_EACH = 144
 RANK = 512
 LAT = 576
-META = 64
-WIDE = LAT + META
+ROT = LAT - RANK
+WIDE = RANK + 2 * ROT
+W_PIECES = 4
 HALF_A = 80
 INV_SEGS = 7282
 
@@ -53,35 +54,43 @@
     return rolled[:, :SEGS_EACH]
 
 
+def parts_of(block):
+    edges = [0, *range(RANK, block.shape[1] + 1, ROT)]
+    return [block[:, a:b] for a, b in zip(edges, edges[1:])]
+
+
 def encode(block):
-    latent, rotary = block[:, :RANK], block[:, RANK:]
-    codes, pieces = [], []
-    for piece in (latent, rotary):
-        top = jnp.max(jnp.abs(piece), axis=1, keepdims=True)
-        code = jnp.ceil(jnp.log2(jnp.maximum(top, 1e-30)) * 128.0 + 0.01)
-        codes.append(code)
-        pieces.append(piece * jnp.exp2(14.999 - code * (1.0 / 128.0)))
-    lane = last_axis_iota(block.shape[0], META)
-    pieces.append(jnp.where(lane < META // 2, codes[0], codes[1]))
-    coded = jnp.concatenate(pieces, axis=1)
-    return jnp.round(coded).astype(jnp.int32).astype(jnp.int16)
-
-
-def decode(coded):
+    n = block.shape[0]
+    diagonal = first_axis_iota(n, 128) == last_axis_iota(n, 128)
+    row_number = first_axis_iota(8, 128)
+    scales = jnp.zeros((8, 128), jnp.float32)
+    pieces = []
+    for i, piece in enumerate(parts_of(block)):
+        top = jnp.maximum(jnp.max(jnp.abs(piece), axis=1, keepdims=True), 1e-30)
+        pieces.append(piece * (32767.0 / top))
+        as_lanes = jnp.sum(jnp.where(diagonal, top, 0.0), axis=0, keepdims=True)
+        scales = jnp.where(row_number == i, as_lanes, scales)
+    coded = pieces[0] if len(pieces) == 1 else jnp.concatenate(pieces, axis=1)
+    return jnp.round(coded).astype(jnp.int32).astype(jnp.int16), scales
+
+
+def decode(coded, scales):
     block = coded.astype(jnp.int32).astype(jnp.float32)
+    n = block.shape[0]
+    diagonal = first_axis_iota(n, 128) == last_axis_iota(n, 128)
     pieces = []
-    for columns, place in ((slice(0, RANK), LAT), (slice(RANK, LAT), LAT + META // 2)):
-        scale = jnp.exp2(block[:, place : place + 1] * (1.0 / 128.0) - 14.999)
-        pieces.append(block[:, columns] * scale)
-    return jnp.concatenate(pieces, axis=1)
+    for i, piece in enumerate(parts_of(block)):
+        top = jnp.sum(jnp.where(diagonal, scales[i : i + 1], 0.0), axis=1, keepdims=True)
+        pieces.append(piece * (top * (1.0 / 32767.0)))
+    return pieces[0] if len(pieces) == 1 else jnp.concatenate(pieces, axis=1)
 
 
 def kernel(
     x_hbm, w_hbm, gain_hbm, page_hbm, length_hbm, start_hbm, freq_hbm, out_ref,
     x_buf, w_buf, gain_buf, page_buf, length_buf, start_buf, freq_buf,
-    part, to_opposite, to_right, to_left, opposite, from_left, from_right,
+    rotary_part, part0, part1, y_send0, y_send1, y_recv0, y_recv1, scale_send, scale_recv,
     z_send0, z_send1, z_recv0, z_recv1, p_send0, p_send1, p_recv0, p_recv1,
-    x_sem, w_sem, i_sem, ys, yr, zs, zr, ps, pr,
+    x_sem, w_sem, i_sem, ys, yr, ss, sr, zs, zr, ps, pr,
 ):
     dec = lax.axis_index("dec")
     tp = lax.axis_index("tp")
@@ -93,6 +102,7 @@
     right = (tp + 1) % TP
     z_send, z_recv = (z_send0, z_send1), (z_recv0, z_recv1)
     p_send, p_recv = (p_send0, p_send1), (p_recv0, p_recv1)
+    part, y_send, y_recv = (part0, part1), (y_send0, y_send1), (y_recv0, y_recv1)
 
     def z_device(zz):
         return xx * (2 * NZ) + zz * 2 + core
@@ -101,14 +111,20 @@
         return (qq // 2) * (2 * NZ) + z * 2 + qq % 2
 
     targets = ((tp + 2) % TP, right, left, tp)
-    w_copy = pltpu.make_async_copy(w_hbm, w_buf, w_sem)
-    w_copy.start()
+    w_rows = LAT // W_PIECES
+    w_copies = [
+        pltpu.make_async_copy(
+            w_hbm.at[pl.ds(i * w_rows, w_rows)], w_buf.at[pl.ds(i * w_rows, w_rows)], w_sem.at[i]
+        )
+        for i in range(W_PIECES)
+    ]
+    for copy in w_copies:
+        copy.start()
     x_copies = [
         pltpu.make_async_copy(x_hbm.at[pl.ds(2 * target, 2)], x_buf.at[i], x_sem.at[i])
         for i, target in enumerate(targets)
     ]
-    for copy in x_copies:
-        copy.start()
+    x_copies[0].start()
     index_copies = [
         pltpu.make_async_copy(src, dst, i_sem.at[i])
         for i, (src, dst) in enumerate(
@@ -142,72 +158,101 @@
 
     lax.fori_loop(1, NZ, greet_z, 0)
     lax.fori_loop(1, NQ, greet_p, 0)
+    for copy in x_copies[1:]:
+        copy.start()
 
     rows_a = pl.ds(0, HALF_A)
     rows_b = pl.ds(HALF_A, SEGS_EACH - HALF_A)
 
     def project(rho, i):
-        return lax.dot_general(
+        result = lax.dot_general(
             x_buf[i, rho], w_buf[...], (((1,), (1,)), ((), ())), preferred_element_type=jnp.float32
         )
-
-    def y_copy(src, dst, rho, kind, target):
-        return pltpu.make_async_remote_copy(
-            src_ref=src,
-            dst_ref=dst,
+        if rho == 0:
+            rotary_part[i] = result[:, RANK:]
+            return result[:, :RANK]
+        return jnp.concatenate([result[:, :RANK], rotary_part[i], result[:, RANK:]], axis=1)
+
+    kinds = (
+        (rows_a, 0, 0, right),
+        (rows_b, 0, 0, left),
+        (rows_b, 1, 1, right),
+        (rows_a, 2, 2, left),
+        (rows_a, 1, 1, right),
+        (rows_b, 2, 2, left),
+    )
+
+    def y_pair(rho, kind):
+        rows, source, place, target = kinds[kind]
+        values = pltpu.make_async_remote_copy(
+            src_ref=y_send[rho].at[source, rows],
+            dst_ref=y_recv[rho].at[place, rows],
             send_sem=ys.at[rho, kind],
             recv_sem=yr.at[rho, kind],
             device_id=(dec, target),
             device_id_type=MESH,
         )
-
-    y_copies = [
-        [
-            y_copy(to_opposite.at[rho, rows_a], opposite.at[rho, rows_a], rho, 0, right),
-            y_copy(to_opposite.at[rho, rows_b], opposite.at[rho, rows_b], rho, 1, left),
-            y_copy(to_right.at[rho, rows_b], from_left.at[rho, rows_b], rho, 2, right),
-            y_copy(to_left.at[rho, rows_a], from_right.at[rho, rows_a], rho, 3, left),
-            y_copy(to_right.at[rho, rows_a], from_left.at[rho, rows_a], rho, 4, right),
-            y_copy(to_left.at[rho, rows_b], from_right.at[rho, rows_b], rho, 5, left),
-        ]
-        for rho in range(2)
-    ]
+        scales = pltpu.make_async_remote_copy(
+            src_ref=scale_send.at[rho, kind],
+            dst_ref=scale_recv.at[rho, kind],
+            send_sem=ss.at[rho, kind],
+            recv_sem=sr.at[rho, kind],
+            device_id=(dec, target),
+            device_id_type=MESH,
+        )
+        return scales, values
+
+    y_copies = [[y_pair(rho, kind) for kind in range(len(kinds))] for rho in range(2)]
+
+    def code(rho, kind, block):
+        rows, source, _, _ = kinds[kind]
+        y_send[rho][source, rows], scale_send[rho, kind] = encode(block)
+
+    def arrived_y(rho, kind):
+        rows, _, place, _ = kinds[kind]
+        for copy in y_copies[rho][kind]:
+            copy.wait_recv()
+        return decode(y_recv[rho][place, rows], scale_recv[rho, kind])
+
+    def project_opposite(rho):
+        result = project(rho, 0)
+        code(rho, 0, result[:HALF_A])
+        code(rho, 1, result[HALF_A:])
 
     def project_right(rho):
         result = project(rho, 1)
-        to_right[rho, rows_b] = encode(result[HALF_A:])
-        part[rho, 1, rows_a] = result[:HALF_A]
+        code(rho, 2, result[HALF_A:])
+        part[rho][1, rows_a] = result[:HALF_A]
 
     def project_left(rho):
         result = project(rho, 2)
-        to_left[rho, rows_a] = encode(result[:HALF_A])
-        part[rho, 2, rows_b] = result[HALF_A:]
-
-    def start(rho, *kinds):
-        for kind in kinds:
-            y_copies[rho][kind].start()
+        code(rho, 3, result[:HALF_A])
+        part[rho][2, rows_b] = result[HALF_A:]
+
+    def start(rho, *which):
+        for kind in which:
+            for copy in y_copies[rho][kind]:
+                copy.start()
 
     def add_and_pass(rho):
-        y_copies[rho][0].wait_recv()
-        to_right[rho, rows_a] = encode(part[rho, 1, rows_a] + decode(opposite[rho, rows_a]))
+        code(rho, 4, part[rho][1, rows_a] + arrived_y(rho, 0))
         start(rho, 4)
-        y_copies[rho][1].wait_recv()
-        to_left[rho, rows_b] = encode(part[rho, 2, rows_b] + decode(opposite[rho, rows_b]))
+        code(rho, 5, part[rho][2, rows_b] + arrived_y(rho, 1))
         start(rho, 5)
 
-    w_copy.wait()
+    for copy in w_copies:
+        copy.wait()
     x_copies[0].wait()
-    to_opposite[0] = encode(project(0, 0))
+    project_opposite(0)
     pl.semaphore_wait(barrier, 2 + (NZ - 1) + (NQ - 1))
     start(0, 0, 1)
     x_copies[1].wait()
     project_right(0)
-    start(0, 2)
     x_copies[2].wait()
     project_left(0)
-    start(0, 3)
+    start(0, 2, 3)
     x_copies[3].wait()
-    part[0, 0] = project(0, 3)
+    part[0][0] = project(0, 3)
 
     for copy in index_copies:
         copy.wait()
@@ -215,10 +260,8 @@
     length_row = own_entries(length_buf, dec)
     start_row = own_entries(start_buf, dec)
     owner_row = (page_row * INV_SEGS) >> 20
-    place_row = page_row - owner_row * SEGS_EACH
     length_col = as_column(length_row.astype(jnp.float32))
     start_col = as_column(start_row.astype(jnp.float32))
-    place_col = as_column(place_row.astype(jnp.float32))
     owner_col = as_column(owner_row.astype(jnp.float32))
     same_owner = owner_col == owner_row.astype(jnp.float32)
     is_earlier = first_axis_iota(SEGS_EACH, SEGS_EACH) < last_axis_iota(SEGS_EACH, SEGS_EACH)
@@ -236,7 +279,6 @@
         jnp.where(first_axis_iota(slots, SEGS_EACH) == row, 1.0, 0.0).astype(jnp.bfloat16)
         for row in slot_rows
     ]
-    meta = jnp.broadcast_to(place_col + 1.0, (SEGS_EACH, META))
 
     by_plane = first_axis_iota(slots, slots)
     by_z = last_axis_iota(slots, slots)
@@ -253,9 +295,11 @@
         angles.append((jnp.cos(phase), jnp.sin(phase)))
 
     add_and_pass(0)
-    to_opposite[1] = encode(project(1, 0))
+    project_opposite(1)
+    start(1, 0, 1)
     project_right(1)
     project_left(1)
+    start(1, 2, 3)
 
     def each_z(act):
         def step(i, carry):
@@ -311,23 +355,29 @@
 
         lax.fori_loop(1, count, step, 0)
 
+    alive = [(2 * tp + rho).astype(jnp.float32) < length_col for rho in range(2)]
+
+    def turn_rotary(rotary, rho):
+        half = ROT // 2
+        front, back = rotary[:, :half], rotary[:, half:]
+        cosine, sine = angles[rho]
+        turned = [front * cosine - back * sine, back * cosine + front * sine]
+        return jnp.where(alive[rho], jnp.concatenate(turned, axis=1), 0.0)
+
     def finish(rho):
-        for kind in (2, 3, 4, 5):
-            y_copies[rho][kind].wait_recv()
-        total = part[rho, 0] + decode(from_left[rho]) + decode(from_right[rho])
+        total_a = part[rho][0, rows_a] + arrived_y(rho, 3) + arrived_y(rho, 4)
+        total_b = part[rho][0, rows_b] + arrived_y(rho, 2) + arrived_y(rho, 5)
+        total = jnp.concatenate([total_a, total_b], axis=0)
         latent = total[:, :RANK]
-        rotary = total[:, RANK:]
         mean_square = jnp.sum(latent * latent, axis=1, keepdims=True) * (1.0 / RANK)
         latent = latent / jnp.sqrt(mean_square + 1e-06) * gain_buf[...]
-        half = (LAT - RANK) // 2
-        front, back = rotary[:, :half], rotary[:, half:]
-        cosine, sine = angles[rho]
-        pieces = [latent, front * cosine - back * sine, back * cosine + front * sine]
-        row = jnp.concatenate(pieces, axis=1)
-        alive = (2 * tp + rho).astype(jnp.float32) < length_col
-        row = jnp.where(alive, row, 0.0)
-        if rho == 0:
-            row = jnp.concatenate([row, meta], axis=1)
+        row = jnp.where(alive[rho], latent, 0.0)
+        if rho == 1:
+            rotaries = [
+                turn_rotary(total[:, RANK : RANK + ROT], 0),
+                turn_rotary(total[:, RANK + ROT :], 1),
+            ]
+            row = jnp.concatenate([row, *rotaries], axis=1)
         return jnp.dot(
             send_tables[rho], row.astype(jnp.bfloat16), preferred_element_type=jnp.float32
         ).astype(jnp.bfloat16)
@@ -354,23 +404,46 @@
         return jnp.dot(table, rows, preferred_element_type=jnp.float32).astype(jnp.bfloat16)
 
     send_z(0, finish(0))
-    start(1, 0, 1, 2, 3)
-    part[1, 0] = project(1, 3)
     add_and_pass(1)
+    part[1][0] = project(1, 3)
     send_p(1, finish(1))
+
+    own_pages = dec * SEGS_EACH + first_axis_iota(SEGS_EACH, 128)
+    lane = last_axis_iota(1, 128)
+
+    def search(i, found):
+        return found + jnp.where(page_buf[pl.ds(i, 1), :] == own_pages, lane + i * 128, 0)
+
+    found = lax.fori_loop(0, SEGS_EACH, search, jnp.zeros((SEGS_EACH, 128), jnp.int32))
+    segment_col = jnp.sum(found.astype(jnp.float32), axis=1, keepdims=True)
+    loader_col = (segment_col.astype(jnp.int32) * INV_SEGS) >> 20
+    loader_row = as_row(loader_col.astype(jnp.float32)).astype(jnp.int32)
+    is_earlier = as_row(segment_col) < segment_col
+    earlier_col = jnp.sum(
+        jnp.where(loader_row == loader_col, jnp.where(is_earlier, 1.0, 0.0), 0.0),
+        axis=1,
+        keepdims=True,
+    ).astype(jnp.int32)
+    loader_plane = (loader_col >> 5) * 2 + (loader_col & 1)
+    loader_z = (loader_col >> 1) & (NZ - 1)
+    slot = last_axis_iota(SEGS_EACH, slots)
+    slot_by_plane = loader_plane * (NZ * CAP) + loader_z * CAP + earlier_col
+    slot_by_z = loader_z * (NQ * CAP) + loader_plane * CAP + earlier_col
+    take_by_plane = jnp.where(slot == slot_by_plane, 1.0, 0.0).astype(jnp.bfloat16)
+    take_by_z = jnp.where(slot == slot_by_z, 1.0, 0.0).astype(jnp.bfloat16)
+
     send_z(1, reorder(to_z_order, arrived_p(1)))
     send_p(0, reorder(to_plane_order, arrived_z(0)))
     landed = arrived_p(0)
-    place = as_row(landed[:, LAT : LAT + 1].astype(jnp.float32))
-    page_ids = (first_axis_iota(SEGS_EACH, slots) + 1).astype(jnp.float32)
-    take_table = jnp.where(page_ids == place, 1.0, 0.0).astype(jnp.bfloat16)
-    out_ref[0] = reorder(take_table, landed[:, :LAT])
-    take_table = reorder(take_table, to_plane_order)
-    out_ref[1] = reorder(take_table, arrived_z(1))
+    out_ref[0, :, :RANK] = reorder(take_by_plane, landed)
+    last = reorder(take_by_z, arrived_z(1))
+    out_ref[0, :, RANK:] = last[:, RANK : RANK + ROT]
+    out_ref[1] = jnp.concatenate([last[:, :RANK], last[:, RANK + ROT :]], axis=1)
 
     for rho in range(2):
-        for copy in y_copies[rho]:
-            copy.wait_send()
+        for pair in y_copies[rho]:
+            for copy in pair:
+                copy.wait_send()
         each_z(lambda other: z_copy(rho, other).wait_send())
         each(NQ, plane, lambda other: p_copy(rho, other).wait_send())
 
@@ -393,24 +466,28 @@
         pltpu.VMEM((n, 128), jnp.int32),
         pltpu.VMEM((n, 128), jnp.int32),
         pltpu.VMEM((1, half), f32),
-        pltpu.VMEM((2, TP - 1, n, LAT), f32),
-        pltpu.VMEM((2, n, WIDE), jnp.int16),
-        pltpu.VMEM((2, n, WIDE), jnp.int16),
-        pltpu.VMEM((2, n, WIDE), jnp.int16),
-        pltpu.VMEM((2, n, WIDE), jnp.int16),
-        pltpu.VMEM((2, n, WIDE), jnp.int16),
-        pltpu.VMEM((2, n, WIDE), jnp.int16),
+        pltpu.VMEM((TP, n, ROT), f32),
+        pltpu.VMEM((TP - 1, n, RANK), f32),
+        pltpu.VMEM((TP - 1, n, WIDE), f32),
+        pltpu.VMEM((TP - 1, n, RANK), jnp.int16),
+        pltpu.VMEM((TP - 1, n, WIDE), jnp.int16),
+        pltpu.VMEM((TP - 1, n, RANK), jnp.int16),
+        pltpu.VMEM((TP - 1, n, WIDE), jnp.int16),
+        pltpu.VMEM((2, 6, 8, 128), f32),
+        pltpu.VMEM((2, 6, 8, 128), f32),
+        pltpu.VMEM((NZ, NQ * CAP, RANK), bf16),
         pltpu.VMEM((NZ, NQ * CAP, WIDE), bf16),
-        pltpu.VMEM((NZ, NQ * CAP, LAT), bf16),
+        pltpu.VMEM((NZ, NQ * CAP, RANK), bf16),
         pltpu.VMEM((NZ, NQ * CAP, WIDE), bf16),
-        pltpu.VMEM((NZ, NQ * CAP, LAT), bf16),
+        pltpu.VMEM((NQ, NZ * CAP, RANK), bf16),
         pltpu.VMEM((NQ, NZ * CAP, WIDE), bf16),
-        pltpu.VMEM((NQ, NZ * CAP, LAT), bf16),
+        pltpu.VMEM((NQ, NZ * CAP, RANK), bf16),
         pltpu.VMEM((NQ, NZ * CAP, WIDE), bf16),
-        pltpu.VMEM((NQ, NZ * CAP, LAT), bf16),
         dma((TP,)),
-        dma(()),
+        dma((W_PIECES,)),
         dma((5,)),
+        dma((2, 6)),
+        dma((2, 6)),
         dma((2, 6)),
         dma((2, 6)),
         dma((2, NZ)),

time: 60.1 us -> 56.5 us (0.940)
  the two profiles are of different devices: /device:TPU:169 before, /device:TPU:193 now
where the time goes in v5:
time: 56.5 us; the launch traced here: 56.3 us
  Pallas kernels  54.6 us (97%)
  local copies, waits for them, and re-layouts  1.76 us (3%)
    pallas_call x1, Pallas kernels, shards(): pl.pallas_call(kernel, out_shape=jax.ShapeDtypeStruct((2, n, LAT), bf16),...  54.6 us
    unnamed x1, local copies, waits for them, and re-layouts  1.76 us

profile of v5, /device:TPU:193, one launch (start us, length us, event | category | flops | bytes accessed | tf_op | source)
XLA Modules:
  0.0 56.3 jit_solution(18322268375415154742)
XLA Ops:
  0.0 54.6 %latent_rows.1 = bf16[2,144,576]{2,1,0:T(8,128)(2,1)} custom-call(bf16[8,144,1792]{2,1,0:T(8,128)(2,1)} %x_hbm.1, bf16[576,1792]{1,0:T(8,128)(2,1)} %bitcast.5, f32[1,512]{1,0:T(1,128)} %bitcast.9, s32[144,128]{1,0:T(8,128)} %bitcast.6, s32[144,128]{1,0:T(8,128)} %bitcast.7, s32[144,128]{1,0:T(8,128)} %bitcast.8, f32[1,32]{1,0:T(1,128)} %constant.2.clone.freq_hbm), custom_call_target="tpu_custom_call" | custom-call | flops 2378170368 | bytes 7000000 | tf_op jit(solution)/shard_map/latent_rows/pallas_call | solution.py:498
  54.6 1.8 %copy.9 = bf16[2,144,576]{2,1,0:T(8,128)(2,1)} copy(bf16[2,144,576]{2,1,0:T(8,128)(2,1)} %latent_rows.1) | data formatting | bytes 663552

commit v6 on v5

--- a/solution.py
+++ b/solution.py
@@ -8,6 +8,7 @@
 from jax.experimental.pallas import tpu as pltpu
 from jax.sharding import PartitionSpec as P
 
+FIRST_PLANES = (7, 7)
 MESH = pl.DeviceIdType.MESH
 TP = 4
 NZ = 16
@@ -88,7 +89,7 @@
 def kernel(
     x_hbm, w_hbm, gain_hbm, page_hbm, length_hbm, start_hbm, freq_hbm, out_ref,
     x_buf, w_buf, gain_buf, page_buf, length_buf, start_buf, freq_buf,
-    rotary_part, part0, part1, y_send0, y_send1, y_recv0, y_recv1, scale_send, scale_recv,
+    part0, part1, y_send0, y_send1, y_recv0, y_recv1, scale_send, scale_recv,
     z_send0, z_send1, z_recv0, z_recv1, p_send0, p_send1, p_recv0, p_recv1,
     x_sem, w_sem, i_sem, ys, yr, ss, sr, zs, zr, ps, pr,
 ):
@@ -164,14 +165,18 @@
     rows_a = pl.ds(0, HALF_A)
     rows_b = pl.ds(HALF_A, SEGS_EACH - HALF_A)
 
+    def times_weight(rows, first, last):
+        return lax.dot_general(
+            rows, w_buf[first:last], (((1,), (1,)), ((), ())), preferred_element_type=jnp.float32
+        )
+
     def project(rho, i):
-        result = lax.dot_general(
-            x_buf[i, rho], w_buf[...], (((1,), (1,)), ((), ())), preferred_element_type=jnp.float32
-        )
-        if rho == 0:
-            rotary_part[i] = result[:, RANK:]
-            return result[:, :RANK]
-        return jnp.concatenate([result[:, :RANK], rotary_part[i], result[:, RANK:]], axis=1)
+        latent = times_weight(x_buf[i, rho], 0, RANK)
+        if rho == 1:
+            return latent
+        both = x_buf[i].reshape(2 * SEGS_EACH, x_buf.shape[-1])
+        rotary = times_weight(both, RANK, LAT)
+        return jnp.concatenate([latent, rotary[:SEGS_EACH], rotary[SEGS_EACH:]], axis=1)
 
     kinds = (
         (rows_a, 0, 0, right),
@@ -308,6 +313,26 @@
 
         lax.fori_loop(0, NZ - 1, step, 0)
 
+    def far_z(first, act):
+        def ahead(i, carry):
+            @pl.when(z != i)
+            def _():
+                act(i)
+
+            return carry
+
+        def others(i, carry):
+            other = (z + NZ // 2 + (1 - 2 * (i % 2)) * ((i + 1) // 2) + NZ) % NZ
+
+            @pl.when(other >= first)
+            def _():
+                act(other)
+
+            return carry
+
+        lax.fori_loop(0, first, ahead, 0)
+        lax.fori_loop(0, NZ - 1, others, 0)
+
     def z_copy(rho, other):
         return pltpu.make_async_remote_copy(
             src_ref=z_send[rho].at[other],
@@ -372,7 +397,7 @@
         mean_square = jnp.sum(latent * latent, axis=1, keepdims=True) * (1.0 / RANK)
         latent = latent / jnp.sqrt(mean_square + 1e-06) * gain_buf[...]
         row = jnp.where(alive[rho], latent, 0.0)
-        if rho == 1:
+        if rho == 0:
             rotaries = [
                 turn_rotary(total[:, RANK : RANK + ROT], 0),
                 turn_rotary(total[:, RANK + ROT :], 1),
@@ -385,7 +410,7 @@
     def send_z(rho, rows):
         z_send[rho][...] = rows.reshape(z_send[rho].shape)
         z_recv[rho][z] = z_send[rho][z]
-        each_z(lambda other: z_copy(rho, other).start())
+        far_z(FIRST_PLANES[rho], lambda other: z_copy(rho, other).start())
 
     def send_p(rho, rows):
         p_send[rho][...] = rows.reshape(p_send[rho].shape)
@@ -435,10 +460,10 @@
     send_z(1, reorder(to_z_order, arrived_p(1)))
     send_p(0, reorder(to_plane_order, arrived_z(0)))
     landed = arrived_p(0)
-    out_ref[0, :, :RANK] = reorder(take_by_plane, landed)
-    last = reorder(take_by_z, arrived_z(1))
-    out_ref[0, :, RANK:] = last[:, RANK : RANK + ROT]
-    out_ref[1] = jnp.concatenate([last[:, :RANK], last[:, RANK + ROT :]], axis=1)
+    first = reorder(take_by_plane, landed)
+    out_ref[0] = first[:, :LAT]
+    out_ref[1, :, RANK:] = first[:, LAT:]
+    out_ref[1, :, :RANK] = reorder(take_by_z, arrived_z(1))
 
     for rho in range(2):
         for pair in y_copies[rho]:
@@ -466,23 +491,22 @@
         pltpu.VMEM((n, 128), jnp.int32),
         pltpu.VMEM((n, 128), jnp.int32),
         pltpu.VMEM((1, half), f32),
-        pltpu.VMEM((TP, n, ROT), f32),
+        pltpu.VMEM((TP - 1, n, WIDE), f32),
         pltpu.VMEM((TP - 1, n, RANK), f32),
-        pltpu.VMEM((TP - 1, n, WIDE), f32),
+        pltpu.VMEM((TP - 1, n, WIDE), jnp.int16),
         pltpu.VMEM((TP - 1, n, RANK), jnp.int16),
         pltpu.VMEM((TP - 1, n, WIDE), jnp.int16),
         pltpu.VMEM((TP - 1, n, RANK), jnp.int16),
-        pltpu.VMEM((TP - 1, n, WIDE), jnp.int16),
         pltpu.VMEM((2, 6, 8, 128), f32),
         pltpu.VMEM((2, 6, 8, 128), f32),
+        pltpu.VMEM((NZ, NQ * CAP, WIDE), bf16),
         pltpu.VMEM((NZ, NQ * CAP, RANK), bf16),
         pltpu.VMEM((NZ, NQ * CAP, WIDE), bf16),
         pltpu.VMEM((NZ, NQ * CAP, RANK), bf16),
-        pltpu.VMEM((NZ, NQ * CAP, WIDE), bf16),
+        pltpu.VMEM((NQ, NZ * CAP, WIDE), bf16),
         pltpu.VMEM((NQ, NZ * CAP, RANK), bf16),
         pltpu.VMEM((NQ, NZ * CAP, WIDE), bf16),
         pltpu.VMEM((NQ, NZ * CAP, RANK), bf16),
-        pltpu.VMEM((NQ, NZ * CAP, WIDE), bf16),
         dma((TP,)),
         dma((W_PIECES,)),
         dma((5,)),

time: 56.5 us -> 56 us (level)
  the two profiles are of different devices: /device:TPU:193 before, /device:TPU:64 now
where the time goes in v6:
time: 56 us; the launch traced here: 55.8 us
  Pallas kernels  54.1 us (97%)
  local copies, waits for them, and re-layouts  1.76 us (3%)
    pallas_call x1, Pallas kernels, shards(): pl.pallas_call(kernel, out_shape=jax.ShapeDtypeStruct((2, n, LAT), bf16),...  54.1 us
    unnamed x1, local copies, waits for them, and re-layouts  1.76 us

profile of v6, /device:TPU:64, one launch (start us, length us, event | category | flops | bytes accessed | tf_op | source)
XLA Modules:
  0.0 55.8 jit_solution(17478027217633110625)
XLA Ops:
  0.0 54.1 %latent_rows.1 = bf16[2,144,576]{2,1,0:T(8,128)(2,1)} custom-call(bf16[8,144,1792]{2,1,0:T(8,128)(2,1)} %x_hbm.1, bf16[576,1792]{1,0:T(8,128)(2,1)} %bitcast.5, f32[1,512]{1,0:T(1,128)} %bitcast.9, s32[144,128]{1,0:T(8,128)} %bitcast.6, s32[144,128]{1,0:T(8,128)} %bitcast.7, s32[144,128]{1,0:T(8,128)} %bitcast.8, f32[1,32]{1,0:T(1,128)} %constant.2.clone.freq_hbm), custom_call_target="tpu_custom_call" | custom-call | flops 2378170368 | bytes 7000000 | tf_op jit(solution)/shard_map/latent_rows/pallas_call | solution.py:522
  54.1 1.8 %copy.9 = bf16[2,144,576]{2,1,0:T(8,128)(2,1)} copy(bf16[2,144,576]{2,1,0:T(8,128)(2,1)} %latent_rows.1) | data formatting | bytes 663552

commit v7 on v6

--- a/solution.py
+++ b/solution.py
@@ -87,11 +87,11 @@
 
 
 def kernel(
-    x_hbm, w_hbm, gain_hbm, page_hbm, length_hbm, start_hbm, freq_hbm, out_ref,
+    x_hbm, w_hbm, gain_hbm, page_hbm, length_hbm, start_hbm, freq_hbm, out_hbm,
     x_buf, w_buf, gain_buf, page_buf, length_buf, start_buf, freq_buf,
     part0, part1, y_send0, y_send1, y_recv0, y_recv1, scale_send, scale_recv,
-    z_send0, z_send1, z_recv0, z_recv1, p_send0, p_send1, p_recv0, p_recv1,
-    x_sem, w_sem, i_sem, ys, yr, ss, sr, zs, zr, ps, pr,
+    z_send0, z_send1, z_recv0, z_recv1, p_send0, p_send1, p_recv0, p_recv1, out_buf,
+    x_sem, w_sem, i_sem, ys, yr, ss, sr, zs, zr, ps, pr, o_sem,
 ):
     dec = lax.axis_index("dec")
     tp = lax.axis_index("tp")
@@ -219,10 +219,19 @@
             copy.wait_recv()
         return decode(y_recv[rho][place, rows], scale_recv[rho, kind])
 
+    def start(rho, *which):
+        for kind in which:
+            for copy in y_copies[rho][kind]:
+                copy.start()
+
     def project_opposite(rho):
         result = project(rho, 0)
         code(rho, 0, result[:HALF_A])
+        if rho == 0:
+            pl.semaphore_wait(barrier, 2 + (NZ - 1) + (NQ - 1))
+        start(rho, 0)
         code(rho, 1, result[HALF_A:])
+        start(rho, 1)
 
     def project_right(rho):
         result = project(rho, 1)
@@ -233,11 +242,6 @@
         result = project(rho, 2)
         code(rho, 3, result[:HALF_A])
         part[rho][2, rows_b] = result[HALF_A:]
-
-    def start(rho, *which):
-        for kind in which:
-            for copy in y_copies[rho][kind]:
-                copy.start()
 
     def add_and_pass(rho):
         code(rho, 4, part[rho][1, rows_a] + arrived_y(rho, 0))
@@ -249,8 +253,6 @@
         copy.wait()
     x_copies[0].wait()
     project_opposite(0)
-    pl.semaphore_wait(barrier, 2 + (NZ - 1) + (NQ - 1))
-    start(0, 0, 1)
     x_copies[1].wait()
     project_right(0)
     x_copies[2].wait()
@@ -301,7 +303,6 @@
 
     add_and_pass(0)
     project_opposite(1)
-    start(1, 0, 1)
     project_right(1)
     project_left(1)
     start(1, 2, 3)
@@ -461,16 +462,21 @@
     send_p(0, reorder(to_plane_order, arrived_z(0)))
     landed = arrived_p(0)
     first = reorder(take_by_plane, landed)
-    out_ref[0] = first[:, :LAT]
-    out_ref[1, :, RANK:] = first[:, LAT:]
-    out_ref[1, :, :RANK] = reorder(take_by_z, arrived_z(1))
+    out_buf[0] = first[:, :LAT]
+    out_copies = [pltpu.make_async_copy(out_buf.at[i], out_hbm.at[i], o_sem.at[i]) for i in range(2)]
+    out_copies[0].start()
+    out_buf[1, :, RANK:] = first[:, LAT:]
 
     for rho in range(2):
         for pair in y_copies[rho]:
             for copy in pair:
                 copy.wait_send()
+        each(NQ, plane, lambda other: p_copy(rho, other).wait_send())
         each_z(lambda other: z_copy(rho, other).wait_send())
-        each(NQ, plane, lambda other: p_copy(rho, other).wait_send())
+    out_buf[1, :, :RANK] = reorder(take_by_z, arrived_z(1))
+    out_copies[1].start()
+    for copy in out_copies:
+        copy.wait()
 
 
 def shards(hidden_rows, compress_weight, latent_gain, segment_page, segment_length, segment_start):
@@ -479,7 +485,6 @@
     frequency = jnp.asarray(np.power(10000.0, -exponent).reshape(1, half).astype(np.float32))
     width = hidden_rows.shape[-1]
     any_spec = pl.BlockSpec(memory_space=pltpu.HBM)
-    vmem_spec = pl.BlockSpec(memory_space=pltpu.VMEM)
     dma = pltpu.SemaphoreType.DMA
     bf16, f32 = jnp.bfloat16, jnp.float32
     n = SEGS_EACH
@@ -507,6 +512,7 @@
         pltpu.VMEM((NQ, NZ * CAP, RANK), bf16),
         pltpu.VMEM((NQ, NZ * CAP, WIDE), bf16),
         pltpu.VMEM((NQ, NZ * CAP, RANK), bf16),
+        pltpu.VMEM((2, n, LAT), bf16),
         dma((TP,)),
         dma((W_PIECES,)),
         dma((5,)),
@@ -518,12 +524,13 @@
         dma((2, NZ)),
         dma((2, NQ)),
         dma((2, NQ)),
+        dma((2,)),
     ]
     return pl.pallas_call(
         kernel,
         out_shape=jax.ShapeDtypeStruct((2, n, LAT), bf16),
         in_specs=[any_spec] * 7,
-        out_specs=vmem_spec,
+        out_specs=any_spec,
         scratch_shapes=scratch,
         compiler_params=pltpu.CompilerParams(
             collective_id=0, has_side_effects=True, vmem_limit_bytes=60 * 1024 * 1024

time: 56 us -> 55.5 us (level)
  Pallas kernels: 54.1 us -> 53.5 us
where the time goes in v7:
time: 55.5 us; the launch traced here: 55.3 us
  Pallas kernels  53.5 us (96%)
  local copies, waits for them, and re-layouts  1.76 us (3%)
    pallas_call x1, Pallas kernels, shards(): pl.pallas_call(kernel, out_shape=jax.ShapeDtypeStruct((2, n, LAT), bf16),...  53.5 us
    unnamed x1, local copies, waits for them, and re-layouts  1.76 us

profile of v7, /device:TPU:64, one launch (start us, length us, event | category | flops | bytes accessed | tf_op | source)
XLA Modules:
  0.0 55.3 jit_solution(9469464920224271473)
XLA Ops:
  0.0 53.5 %latent_rows.1 = bf16[2,144,576]{2,1,0:T(8,128)(2,1)} custom-call(bf16[8,144,1792]{2,1,0:T(8,128)(2,1)} %x_hbm.1, bf16[576,1792]{1,0:T(8,128)(2,1)} %bitcast.5, f32[1,512]{1,0:T(1,128)} %bitcast.9, s32[144,128]{1,0:T(8,128)} %bitcast.6, s32[144,128]{1,0:T(8,128)} %bitcast.7, s32[144,128]{1,0:T(8,128)} %bitcast.8, f32[1,32]{1,0:T(1,128)} %constant.2.clone.freq_hbm), custom_call_target="tpu_custom_call" | custom-call | flops 2378170368 | bytes 7000000 | tf_op jit(solution)/shard_map/latent_rows/pallas_call | solution.py:529
  53.6 1.8 %copy.9 = bf16[2,144,576]{2,1,0:T(8,128)(2,1)} copy(bf16[2,144,576]{2,1,0:T(8,128)(2,1)} %latent_rows.1) | data formatting | bytes 663552
